TPU v7x, 512 devices: a whole 4x8x8 slice. The times are simulated.
512 devices in a mesh: row: 64 (over z, x, core), col: 8 (over y).
Axes of the slice: x: 4, y: 8, z: 8, core: 2. Of those that a mesh axis runs over, the one named last changes fastest.
Arguments:
- noise: bfloat16 [32768, 512], P('row', 'col'), may hold values from -7 to 7
- data: bfloat16 [16384, 512], P(('col', 'row')), may hold values from -7 to 7
Outputs:
- targets: bfloat16 [32768, 512], P('row', 'col')
All inputs are finite; a program needn't handle non-finite values.
Results may differ from a plain program's by a relative error of at most 0.015.
Values may be sent and summed in bfloat16 or wider, within the bound.
No kernel may reach another device: no remote copies, remote signals or barrier semaphores. Data moves between devices by JAX's collectives and lax.ppermute only.
A program may use at most 64 MiB of HBM per device.

v0:
```python
import math

import jax
import jax.numpy as jnp
from jax import lax
from jax.sharding import PartitionSpec as P

ITERS = 4


eps_reg = 0.01


def cost_tile(rows, rows_sq, piece):
    cross = jnp.dot(rows, piece.T, preferred_element_type=jnp.float32)
    piece_f = piece.astype(jnp.float32)
    piece_sq = jnp.sum(piece_f * piece_f, axis=1)
    return (rows_sq[:, None] + piece_sq[None, :] - 2.0 * cross) / rows.shape[1]


def on_device(noise, data):
    noise_all = lax.all_gather(noise, "col", axis=1, tiled=True)
    noise_f = noise_all.astype(jnp.float32)
    noise_sq = jnp.sum(noise_f * noise_f, axis=1)
    data_all = lax.all_gather(data, "row", axis=0, tiled=True)
    cost = cost_tile(noise_all, noise_sq, data_all)
    rows_here, cols_here = cost.shape
    log_noise = math.log(rows_here * lax.axis_size("row"))
    log_data = math.log(cols_here * lax.axis_size("col"))
    f_pot = jnp.zeros((rows_here,), jnp.float32)
    row_lse = jnp.zeros((rows_here,), jnp.float32)
    scores = cost
    for sweep in range(ITERS):
        scores = (f_pot[:, None] - cost) / eps_reg
        local_top = jnp.max(scores, axis=0)
        top = lax.pmax(local_top, "row")
        total = lax.psum(jnp.sum(jnp.exp(scores - top[None, :]), axis=0), "row")
        g_pot = -eps_reg * log_data - eps_reg * (top + jnp.log(total))
        scores = (g_pot[None, :] - cost) / eps_reg
        local_peak = jnp.max(scores, axis=1)
        peak = lax.pmax(local_peak, "col")
        mass = lax.psum(jnp.sum(jnp.exp(scores - peak[:, None]), axis=1), "col")
        row_lse = peak + jnp.log(mass)
        f_pot = -eps_reg * log_noise - eps_reg * row_lse
    weights = jnp.exp(scores - row_lse[:, None]).astype(jnp.bfloat16)
    partial_sums = jnp.dot(weights, data_all, preferred_element_type=jnp.float32)
    return lax.psum_scatter(
        partial_sums.astype(jnp.bfloat16), "col", scatter_dimension=1, tiled=True
    )


def solution(mesh):
    return jax.shard_map(
        on_device,
        mesh=mesh,
        in_specs=(P("row", "col"), P(("col", "row"), None)),
        out_specs=P("row", "col"),
        check_vma=False,
    )
```

profile of v0, /device:TPU:1, one launch (start us, length us, event | category | flops | bytes accessed | tf_op | source)
XLA Modules:
  0.0 1327.1 jit_solution(6178438454959372418)
XLA Ops:
  6.5 0.0 all-gather.2.cloned.1.call-start
  6.5 0.7 all-gather.2.cloned.1.call-update
  7.3 0.0 reduce-scatter.2.cloned.1.call-start
  7.3 21.9 %all_gather.6 = bf16[512,512]{0,1:T(8,128)(2,1)S(1)} all-gather(bf16[512,64]{0,1:T(8,128)(2,1)} %param.2), channel_id=1, replica_groups=mesh['row'=64,'col'=8] {'col'}, dimensions={1}, use_global_device_ids=true | all-gather | bytes 589824 | tf_op jit(solution)/shard_map/all_gather | solution.py:22
  29.2 0.2 multiply_reduce_fusion.1
  29.4 70.6 %all-gather.2.cloned.1.call-done = bf16[2048,512]{1,0:T(8,128)(2,1)} async-done(((bf16[32,512]{1,0:T(8,128)(2,1)}), bf16[2048,512]{1,0:T(8,128)(2,1)}) %all-gather.2.cloned.1.call-update) | async-done | bytes 2097168 | tf_op jit(solution)/shard_map/all_gather | solution.py:25
  100.0 2.1 multiply_reduce_fusion
  102.1 5.7 fusion
  107.8 125.6 %pmax.56 = f32[2048]{0:T(1024)S(1)} all-reduce(f32[2048]{0:T(1024)S(1)} %get-tuple-element.5), channel_id=1, replica_groups=mesh['row'=64,'col'=8] {'row'}, use_global_device_ids=true, to_apply=%region_3.0 | all-reduce | flops 2048 | bytes 16384 | tf_op jit(solution)/shard_map/pmax | solution.py:36
  233.4 3.0 exponential_reduce_fusion.7
  236.4 128.7 %psum.56 = f32[2048]{0:T(1024)S(1)} all-reduce(f32[2048]{0:T(1024)S(1)} %exponential_reduce_fusion.7), channel_id=1, replica_groups=mesh['row'=64,'col'=8] {'row'}, use_global_device_ids=true, to_apply=%region_5.0 | all-reduce | flops 2048 | bytes 16384 | tf_op jit(solution)/shard_map/psum | solution.py:37
  365.1 2.7 fusion.1
  367.8 13.2 pmax.57
  381.0 3.1 exponential_reduce_fusion.6
  384.1 11.6 psum.57
  395.8 2.7 fusion.2
  398.5 133.4 %pmax.58 = f32[2048]{0:T(1024)S(1)} all-reduce(f32[2048]{0:T(1024)S(1)} %fusion.2), channel_id=1, replica_groups=mesh['row'=64,'col'=8] {'row'}, use_global_device_ids=true, to_apply=%region_11.0 | all-reduce | flops 2048 | bytes 16384 | tf_op jit(solution)/shard_map/pmax | solution.py:36
  531.9 3.1 exponential_reduce_fusion.5
  535.0 126.1 %psum.58 = f32[2048]{0:T(1024)S(1)} all-reduce(f32[2048]{0:T(1024)S(1)} %exponential_reduce_fusion.5), channel_id=1, replica_groups=mesh['row'=64,'col'=8] {'row'}, use_global_device_ids=true, to_apply=%region_13.0 | all-reduce | flops 2048 | bytes 16384 | tf_op jit(solution)/shard_map/psum | solution.py:37
  661.1 2.7 fusion.3
  663.8 11.3 pmax.59
  675.1 3.1 exponential_reduce_fusion.4
  678.3 11.6 psum.59
  689.9 2.7 fusion.4
  692.6 133.4 %pmax.60 = f32[2048]{0:T(1024)S(1)} all-reduce(f32[2048]{0:T(1024)S(1)} %fusion.4), channel_id=1, replica_groups=mesh['row'=64,'col'=8] {'row'}, use_global_device_ids=true, to_apply=%region_19.0 | all-reduce | flops 2048 | bytes 16384 | tf_op jit(solution)/shard_map/pmax | solution.py:36
  826.0 3.1 exponential_reduce_fusion.3
  829.1 126.1 %psum.60 = f32[2048]{0:T(1024)S(1)} all-reduce(f32[2048]{0:T(1024)S(1)} %exponential_reduce_fusion.3), channel_id=1, replica_groups=mesh['row'=64,'col'=8] {'row'}, use_global_device_ids=true, to_apply=%region_21.0 | all-reduce | flops 2048 | bytes 16384 | tf_op jit(solution)/shard_map/psum | solution.py:37
  955.3 2.7 fusion.5
  957.9 11.5 pmax.61
  969.5 3.1 exponential_reduce_fusion.2
  972.6 11.6 psum.61
  984.2 2.7 fusion.6
  986.9 133.4 %pmax.62 = f32[2048]{0:T(1024)S(1)} all-reduce(f32[2048]{0:T(1024)S(1)} %fusion.6), channel_id=1, replica_groups=mesh['row'=64,'col'=8] {'row'}, use_global_device_ids=true, to_apply=%region_27.0 | all-reduce | flops 2048 | bytes 16384 | tf_op jit(solution)/shard_map/pmax | solution.py:36
  1120.4 3.1 exponential_reduce_fusion.1
  1123.4 126.1 %psum.62 = f32[2048]{0:T(1024)S(1)} all-reduce(f32[2048]{0:T(1024)S(1)} %exponential_reduce_fusion.1), channel_id=1, replica_groups=mesh['row'=64,'col'=8] {'row'}, use_global_device_ids=true, to_apply=%region_29.0 | all-reduce | flops 2048 | bytes 16384 | tf_op jit(solution)/shard_map/psum | solution.py:37
  1249.6 0.0 copy-start
  1249.6 2.8 fusion.7
  1252.4 11.3 pmax.63
  1263.7 3.1 exponential_reduce_fusion
  1266.8 11.6 psum.63
  1278.5 0.0 copy-done
  1278.5 4.5 fusion.12
  1283.0 0.0 reduce-scatter.2.cloned.1.call-update
  1283.0 37.2 %reduce-scatter.2.cloned.1.call-done = bf16[512,64]{0,1:T(8,128)(2,1)} async-done(((bf16[512,512]{0,1:T(8,128)(2,1)}), bf16[512,64]{0,1:T(8,128)(2,1)}) %reduce-scatter.2.cloned.1.call-update) | async-done | bytes 65552 | tf_op jit(solution)/shard_map/reduce_scatter | solution.py:47
  (8 shorter events, 0.1 us)
Async XLA Ops:
  6.5 93.5 %all-gather.2.cloned.1.call-start = ((), (), s32[]{:S(2)}) async-start(), calls=%async_computation.1 | async-start | bytes 2129920 | tf_op jit(solution)/shard_map/all_gather | solution.py:25
  7.3 1313.0 %reduce-scatter.2.cloned.1.call-start = ((), (), s32[]{:S(2)}) async-start(), calls=%async_computation.2 | async-start | bytes 589824 | tf_op jit(solution)/shard_map/reduce_scatter | solution.py:47
  1249.6 28.9 %copy-start = (bf16[2048,512]{1,0:T(8,128)(2,1)S(1)}, bf16[2048,512]{1,0:T(8,128)(2,1)}, u32[]{:S(2)}) copy-start(bf16[2048,512]{1,0:T(8,128)(2,1)} %all-gather.2.cloned.1.call-done) | copy-start | bytes 6291460
Sparse Core Ops, SparseCore 0:
  10.7 89.2 all-gather.1
  1283.1 37.0 reduce-scatter.1
where the time goes:
time: 1330 us
  blocking collectives  1150 us (86%)
  waiting for transfers between devices  109 us (8%)
  other arithmetic  45.9 us (3%)
  between operations  13.6 us (1%)
    pmax x4, blocking collectives, on_device(): top = lax.pmax(local_top, 'row')  526 us
    psum x4, blocking collectives, on_device(): total = lax.psum(jnp.sum(jnp.exp(scores - top[None, :]), axis=0), 'row')  507 us
    all_gather x1, waiting for transfers between devices, on_device(): data_all = lax.all_gather(data, 'row', axis=0, tiled=True)  70.6 us
    pmax x4, blocking collectives, on_device(): peak = lax.pmax(local_peak, 'col')  47.4 us
    psum x4, blocking collectives, on_device(): mass = lax.psum(jnp.sum(jnp.exp(scores - peak[:, None]), axis=1), 'col')  46.6 us
    reduce_scatter x1, waiting for transfers between devices, on_device(): lax.psum_scatter(partial_sums.astype(jnp.bfloat16), 'col', scatter_dimens...  37.2 us
  transfers between devices with their start and end apart: 2, of which 2 were waited for; matrix products, arithmetic and copies ran while one was open for 0% of the time, Pallas kernels for 0%

commit v1 on v0

v1 whole, which is shorter than its diff:
```python
import functools
import math

import jax
import jax.numpy as jnp
from jax import lax
from jax.experimental import pallas as pl
from jax.experimental.pallas import tpu as pltpu
from jax.sharding import PartitionSpec as P

ITERS = 4
EPS = 0.01
CORES, XS = 2, 4
SHIFT = 24.0 * math.log(2.0)
SCALE = 2.0**48
F32, BF16 = jnp.float32, jnp.bfloat16
VM = pl.BlockSpec(memory_space=pltpu.VMEM)


def params(mib):
    return pltpu.CompilerParams(vmem_limit_bytes=mib * 2**20)


def in_vmem(shape, dtype):
    return pltpu.VMEM(shape, dtype)


def call(body, outs, count, scratch=(), mib=32, name=None):
    return pl.pallas_call(
        body,
        out_shape=outs,
        in_specs=[VM] * count,
        out_specs=jax.tree.map(lambda _: VM, outs, is_leaf=lambda o: hasattr(o, "dtype")),
        scratch_shapes=list(scratch),
        compiler_params=params(mib),
        name=name,
    )


def lanes_to_rows(vec, out_ref):
    for r in range(vec.shape[0]):
        block = jnp.broadcast_to(vec[r : r + 1, :], (128, 128))
        out_ref[r * 128 : (r + 1) * 128, :] = block.T


def rows_to_lanes(ref):
    parts = []
    for r in range(ref.shape[0] // 128):
        parts.append(jnp.sum(ref[r * 128 : (r + 1) * 128, :].T, axis=0, keepdims=True))
    return jnp.concatenate(parts, axis=0)


def flat(vec):
    return jnp.concatenate([vec[t : t + 1, :] for t in range(vec.shape[0])], axis=1)


def lane_sum(val):
    total = val[:, 0:128]
    for t in range(1, val.shape[1] // 128):
        total = total + val[:, t * 128 : (t + 1) * 128]
    return total


def parts_of(refs):
    parts = []
    for ref in refs:
        if len(ref.shape) == 3:
            parts += [ref[k] for k in range(ref.shape[0])]
        else:
            parts.append(ref[...])
    return parts


def merged(refs):
    parts = parts_of(refs)
    top = functools.reduce(jnp.maximum, parts)
    return top + jnp.log(sum(jnp.exp(part - top) for part in parts))


def added(refs):
    return functools.reduce(jnp.add, parts_of(refs))


def noise_body(parts, out):
    for r in range(out.shape[0] // 128):
        at = slice(r * 128, (r + 1) * 128)
        block = jnp.concatenate(
            [parts[k, :, at].astype(F32).T for k in range(parts.shape[0])], axis=1
        )
        out[at, :] = block.astype(BF16)


def half_at(flip, rows):
    return pl.multiple_of(lax.rem(lax.axis_index("c") + flip, 2) * rows, rows)


def cost_body(own, far, data, score, lse, sq):
    rows, depth = own.shape
    width = 256
    ones = jnp.ones((8, depth), BF16)
    contract = (((1,), (1,)), ((), ()))
    for flip, noise in enumerate((own, far)):
        for r in range(rows // 128):
            block = noise[r * 128 : (r + 1) * 128, :].astype(F32)
            total = jnp.sum(lane_sum(block * block), axis=1, keepdims=True)
            sq[flip, r * 128 : (r + 1) * 128, :] = jnp.broadcast_to(total, (128, 128))
    for b in range(data.shape[0] // width):
        at = slice(b * width, (b + 1) * width)
        piece = data[at, :]
        wide = piece.astype(F32)
        square = wide * wide
        high = square.astype(BF16)
        low = (square - high.astype(F32)).astype(BF16)
        piece_sq = lax.dot_general(ones, high, contract, preferred_element_type=F32)
        piece_sq += lax.dot_general(ones, low, contract, preferred_element_type=F32)
        vals, tops = [], []
        for flip, noise in enumerate((own, far)):
            cross = lax.dot_general(noise[...], piece, contract, preferred_element_type=F32)
            rows_sq = jnp.concatenate([sq[flip]] * (width // 128), axis=1)
            val = (2.0 * cross - rows_sq - piece_sq[0:1, :]) * (1.0 / (depth * EPS))
            score[pl.ds(half_at(flip, rows), rows), at] = val
            vals.append(val)
            tops.append(jnp.max(val, axis=0, keepdims=True))
        top = jnp.maximum(tops[0], tops[1])
        total = sum(jnp.sum(jnp.exp(val - top), axis=0, keepdims=True) for val in vals)
        part = top + jnp.log(total)
        for t in range(width // 128):
            row = b * (width // 128) + t
            lse[row : row + 1, :] = part[:, t * 128 : (t + 1) * 128]


def first_row_body(log_data, n, *refs):
    parts, (score, expd, peak, lse, part, tops) = refs[:n], refs[n:]
    pot = flat(-log_data - merged(parts))
    rows = expd.shape[0]
    step = 32

    def body(r, carry):
        at = pl.ds(pl.multiple_of(r * step, step), step)
        val = score[at, :] + pot
        top = jnp.max(val, axis=1, keepdims=True)
        e = jnp.exp(val - (top - SHIFT))
        expd[at, :] = e
        part[at, :] = lane_sum(e)
        tops[at, :] = jnp.broadcast_to(top, (step, 128))
        return carry

    lax.fori_loop(0, rows // step, body, 0)
    sums = rows_to_lanes(part)
    high = jnp.concatenate(
        [tops[r * 128 : (r + 1) * 128, :].T[0:1, :] for r in range(rows // 128)], axis=0
    )
    peak[...] = high
    lse[...] = high + (jnp.log(sums) - SHIFT)


def column_sums(expd, factor, factors, out):
    lanes_to_rows(factor, factors)
    rows, cols = expd.shape
    copies = cols // 128

    def body(r, acc):
        at = pl.ds(pl.multiple_of(r * 8, 8), 8)
        f = factors[at, :]
        return acc + expd[at, :] * jnp.concatenate([f] * copies, axis=1)

    acc = lax.fori_loop(0, rows // 8, body, jnp.zeros((8, cols), F32), unroll=4)
    sums = jnp.sum(acc, axis=0, keepdims=True)
    count, width = out.shape
    for t in range(count):
        out[t : t + 1, :] = sums[:, t * width : (t + 1) * width]


def first_col_body(count, n, *refs):
    parts, (peak, expd, out, scale, factor, factors) = refs[:n], refs[n:]
    lse = merged(parts)
    s = jnp.exp(peak[...] - lse + SHIFT)
    scale[...] = s
    f = s * (1.0 / count)
    factor[...] = f
    column_sums(expd, f, factors, out)


def col_body(count, n, *refs):
    parts, (scale, expd, out, factor, factors) = refs[:n], refs[n:]
    f = scale[...] * ((SCALE / count) / added(parts))
    factor[...] = f
    column_sums(expd, f, factors, out)


def row_body(count, n, *refs):
    parts, (scale, expd, out, part) = refs[:n], refs[n:]
    v = jnp.broadcast_to(flat((SCALE / count) / added(parts)), (8, expd.shape[1]))
    rows = expd.shape[0]

    def body(r, carry):
        at = pl.ds(pl.multiple_of(r * 8, 8), 8)
        part[at, :] = lane_sum(expd[at, :] * v)
        return carry

    lax.fori_loop(0, rows // 8, body, 0, unroll=4)
    out[...] = rows_to_lanes(part) * scale[...]


def split_three(mass, deep):
    high = mass.astype(BF16)
    rest = mass - high.astype(F32)
    mid = rest.astype(BF16)
    low = (rest - mid.astype(F32)).astype(BF16)
    zero = jnp.zeros((deep - 3, mass.shape[1]), BF16)
    return jnp.concatenate([high, mid, low, zero], axis=0)


def add_three(tail):
    return tail[0:1, :] + tail[1:2, :] + tail[2:3, :]


def target_body(count, flip, n, *refs):
    parts, (factor, expd, data, out) = refs[:n], refs[n : n + 4]
    *mass, part, factors, weights = refs[n + 4 :]
    v = jnp.broadcast_to(flat((SCALE / count) / added(parts)), (16, expd.shape[1]))
    rows, wide = weights.shape
    base = half_at(flip, rows)
    lanes_to_rows(factor[pl.ds(lax.rem(lax.axis_index("c") + flip, 2) * (rows // 128), rows // 128), :], factors)

    def body(r, carry):
        at = pl.ds(pl.multiple_of(r * 16, 16), 16)
        f = jnp.concatenate([factors[at, :]] * (wide // 128), axis=1)
        w = expd[pl.ds(pl.multiple_of(base + r * 16, 16), 16), :] * v * f
        part[at, :] = lane_sum(w)
        weights[at, :] = w.astype(BF16)
        return carry

    lax.fori_loop(0, rows // 16, body, 0, unroll=2)
    cols, deep, _ = out.shape
    depth = data.shape[1] // cols
    for r in range(rows // 128):
        at = slice(r * 128, (r + 1) * 128)
        block = jnp.dot(weights[at, :], data[...], preferred_element_type=F32)
        block = block.T.astype(out.dtype)
        for k in range(cols):
            out[k, 0:depth, at] = block[k * depth : (k + 1) * depth, :]
    sums = rows_to_lanes(part)
    if mass:
        mass[0][...] = sums
    else:
        tail = split_three(flat(sums), deep - depth)
        for k in range(cols):
            out[k, depth:deep, :] = tail


def pack_body(own, mass, far, out):
    depth, deep = own.shape[1], out.shape[1]
    total = flat(mass[...]) + add_three(far[0, depth:deep, :].astype(F32))
    tail = split_three(total, deep - depth)
    for k in range(out.shape[0]):
        out[k, 0:depth, :] = (own[k] + far[k, 0:depth, :].astype(F32)).astype(BF16)
        out[k, depth:deep, :] = tail


def finish_body(parts, out):
    depth, deep = out.shape[0], parts.shape[1]
    total = functools.reduce(jnp.add, [parts[k, 0:depth, :].astype(F32) for k in range(parts.shape[0])])
    tails = [parts[k, depth:deep, :].astype(F32) for k in range(parts.shape[0])]
    out[...] = (total / add_three(functools.reduce(jnp.add, tails))).astype(BF16)


def everyone(val, axes):
    count = lax.axis_size(axes)
    copies = jnp.broadcast_to(val[None], (count,) + val.shape)
    return lax.all_to_all(copies, axes, 0, 0, tiled=True)


def swapped(val):
    return lax.ppermute(val, "c", [(0, 1), (1, 0)])


def on_device(noise, data, *, vmem=in_vmem):
    zs, xs, cs, cols_all = (lax.axis_size(a) for a in ("z", "x", "c", "col"))
    half, slice_width = noise.shape
    rows = half * cs
    depth = slice_width * cols_all
    wide = data.shape[0] * zs * xs
    count_noise, count_data = float(rows * zs * xs), float(wide * cs * cols_all)
    log_data = math.log(count_data)
    row_axes, col_axes = ("z", "x"), ("col", "c")

    noise_parts = lax.all_gather(noise.T, "col", axis=0)
    stacked = everyone(data, "z").reshape(data.shape[0] * zs, depth)
    data_all = everyone(stacked, "x").reshape(wide, depth)
    own = call(noise_body, jax.ShapeDtypeStruct((half, depth), BF16), 1, name="noise")(noise_parts)
    far = swapped(own)

    vec_col = jax.ShapeDtypeStruct((wide // 128, 128), F32)
    vec_row = jax.ShapeDtypeStruct((rows // 128, 128), F32)
    tile = vmem((rows, wide), F32)
    strip = pltpu.VMEM((rows, 128), F32)

    score, lse = call(
        cost_body, (tile, vec_col), 3, [pltpu.VMEM((cs, half, 128), F32)], name="cost"
    )(own, far, data_all)
    parts = everyone(lse, row_axes)
    expd, peak, lse = call(
        functools.partial(first_row_body, log_data, 1),
        (tile, vec_row, vec_row), 2, [strip, strip], name="first_rows",
    )(parts, score)
    parts = everyone(lse, col_axes)
    sums, scale, factor = call(
        functools.partial(first_col_body, count_noise, 1),
        (vec_col, vec_row, vec_row), 3, [strip], name="first_cols",
    )(parts, peak, expd)
    for sweep in range(1, ITERS - 1):
        parts = everyone(sums, row_axes)
        mass = call(
            functools.partial(row_body, count_data, 1), vec_row, 3, [strip], name="rows"
        )(parts, scale, expd)
        parts = everyone(mass, col_axes)
        sums, factor = call(
            functools.partial(col_body, count_noise, 1), (vec_col, vec_row), 3, [strip], name="cols"
        )(parts, scale, expd)
    parts = everyone(sums, row_axes)

    strips = [pltpu.VMEM((half, 128), F32)] * 2 + [pltpu.VMEM((half, wide), BF16)]
    packed = jax.ShapeDtypeStruct((cols_all, slice_width + 16, half), BF16)
    far = call(
        functools.partial(target_body, count_data, 1, 1), packed, 4, strips, name="targets_far"
    )(parts, factor, expd, data_all)
    far = swapped(far)
    mine, mass = call(
        functools.partial(target_body, count_data, 0, 1),
        (vmem((cols_all, slice_width, half), F32), jax.ShapeDtypeStruct((half // 128, 128), F32)),
        4, strips, name="targets_own",
    )(parts, factor, expd, data_all)
    pieces = call(pack_body, packed, 3, name="pack")(mine, mass, far)
    got = lax.all_to_all(pieces, "col", 0, 0, tiled=True)
    out = call(finish_body, jax.ShapeDtypeStruct((slice_width, half), BF16), 1, name="finish")(got)
    return out.T


def solution(mesh):
    rows, cols = mesh.devices.shape
    parts = (rows // (XS * CORES), XS, CORES, cols)
    split = jax.sharding.Mesh(mesh.devices.reshape(parts), ("z", "x", "c", "col"))
    return jax.shard_map(
        on_device,
        mesh=split,
        in_specs=(P(("z", "x", "c"), "col"), P(("col", "z", "x", "c"), None)),
        out_specs=P(("z", "x", "c"), "col"),
        check_vma=False,
    )
```

time: 1330 us -> 195 us (0.15)
  blocking collectives: 1150 us -> 158 us
  waiting for transfers between devices: 109 us -> 1.85 us
  other arithmetic: 45.9 us -> 0 us
  starting transfers between devices: 0.04 us -> 17.2 us
  Pallas kernels: 0 us -> 15.4 us
  between operations: 13.6 us -> 0.12 us
    pmax x8 -> x0, blocking collectives: 573 us -> none  [the longest x4 526 us: on_device(): top = lax.pmax(local_top, 'row')]
    psum x8 -> x0, blocking collectives: 554 us -> none  [the longest x4 507 us: on_device(): total = lax.psum(jnp.sum(jnp.exp(scores - top[None, :]), axis=0), 'row')]
    all_to_all x0 -> x9, blocking collectives: none -> 136 us  [the longest x8 113 us: everyone(): return lax.all_to_all(copies, axes, 0, 0, tiled=True)]
    all_gather x1 -> x0, waiting for transfers between devices: 70.6 us -> none  [on_device(): data_all = lax.all_gather(data, 'row', axis=0, tiled=True)]
    reduce_scatter x1 -> x0, waiting for transfers between devices: 37.2 us -> none  [on_device(): lax.psum_scatter(partial_sums.astype(jnp.bfloat16), 'col', scatter_dimens...]
    reduce_sum x10 -> x0, other arithmetic: 27 us -> none  [the longest x4 12.5 us: on_device(): mass = lax.psum(jnp.sum(jnp.exp(scores - peak[:, None]), axis=1), 'col')]
    reduce_max x7 -> x0, other arithmetic: 18.9 us -> none  [the longest x4 10.8 us: on_device(): local_peak = jnp.max(scores, axis=1)]
    pallas_call x0 -> x12, Pallas kernels: none -> 15.4 us  [the longest x1 3.99 us: on_device(): call(functools.partial(first_row_body, log_data, 1), (tile, vec_row, vec_...]
  transfers between devices with their start and end apart: 2 -> 3, of which waited for: 2 -> 2; matrix products, arithmetic and copies ran while one was open for 0% -> 0% of each run, Pallas kernels for 0% -> 1%
where the time goes in v1:
time: 195 us; the launch traced here: 194 us
  blocking collectives  158 us (81%)
  starting transfers between devices  17.2 us (9%)
  Pallas kernels  15.4 us (8%)
    all_to_all x8, blocking collectives, everyone(): return lax.all_to_all(copies, axes, 0, 0, tiled=True)  113 us
    all_to_all x1, blocking collectives, on_device(): got = lax.all_to_all(pieces, 'col', 0, 0, tiled=True)  23.2 us
    all_gather x1, blocking collectives, on_device(): noise_parts = lax.all_gather(noise.T, 'col', axis=0)  21.8 us
    ppermute x2, starting transfers between devices, swapped(): return lax.ppermute(val, 'c', [(0, 1), (1, 0)])  13.1 us
    all_to_all x1, starting transfers between devices, everyone(): return lax.all_to_all(copies, axes, 0, 0, tiled=True)  4.01 us
    pallas_call x1, Pallas kernels, on_device(): call(functools.partial(first_row_body, log_data, 1), (tile, vec_row, vec_...  3.99 us
  transfers between devices with their start and end apart: 3, of which 2 were waited for; matrix products, arithmetic and copies ran while one was open for 0% of the time, Pallas kernels for 1%

profile of v1, /device:TPU:1, one launch (start us, length us, event | category | flops | bytes accessed | tf_op | source)
XLA Modules:
  0.0 194.3 jit_solution(206190133378640375)
XLA Ops:
  0.0 0.0 copy-start
  0.0 0.8 broadcast_in_dim.20
  0.8 21.0 %all_to_all.50 = bf16[8,32,512]{2,1,0:T(8,128)(2,1)S(1)} all-to-all(bf16[8,32,512]{2,1,0:T(8,128)(2,1)S(1)} %broadcast_in_dim.20), channel_id=1, replica_groups=mesh['z'=8,'x'=4,'c'=2,'col'=8] {'z'}, dimensions={0} | all-to-all | bytes 524288 | tf_op jit(solution)/shard_map/all_to_all | solution.py:271
  21.8 1.1 broadcast_in_dim.22
  22.9 4.0 %all-to-all-start.1 = ((bf16[4,256,512]{2,1,0:T(8,128)(2,1)}), bf16[4,256,512]{2,1,0:T(8,128)(2,1)S(1)}, u32[]{:S(2)}, u32[]{:S(2)}) async-start(bf16[4,256,512]{2,1,0:T(8,128)(2,1)} %broadcast_in_dim.22), calls=%async_computation.1 | async-start | bytes 2097152 | tf_op jit(solution)/shard_map/all_to_all | solution.py:271
  26.9 0.0 copy-done
  26.9 21.8 %all-gather = bf16[512,512]{1,0:T(8,128)(2,1)S(1)} all-gather(bf16[64,512]{1,0:T(8,128)(2,1)S(1)} %bitcast.10), channel_id=2, replica_groups=mesh['z'=8,'x'=4,'c'=2,'col'=8] {'col'}, dimensions={0}, use_global_device_ids=true | all-gather | bytes 589824 | tf_op jit(solution)/shard_map/all_gather | solution.py:288
  48.7 0.5 noise.1.own
  49.2 9.7 %collective-permute-start = (bf16[512,512]{1,0:T(8,128)(2,1)S(1)}, bf16[512,512]{1,0:T(8,128)(2,1)S(1)}, u32[]{:S(2)}, u32[]{:S(2)}) collective-permute-start(bf16[512,512]{1,0:T(8,128)(2,1)S(1)} %noise.1.own), channel_id=1, source_target_pairs={{0,8},{8,0},{1,9},{9,1},{2,10},{10,2},{3,11},{11,3},{4,12},{12,4},... | collective-permute-start | bytes 1572872 | tf_op jit(solution)/shard_map/ppermute | solution.py:275
  58.9 1.5 collective-permute-done.far
  60.4 0.0 all-to-all-done.1
  60.4 2.7 %cost.1 = (f32[1024,1024]{1,0:T(8,128)S(1)}, f32[8,128]{1,0:T(8,128)S(1)}) custom-call(bf16[512,512]{1,0:T(8,128)(2,1)S(1)} %noise.1.own, bf16[512,512]{1,0:T(8,128)(2,1)S(1)} %collective-permute-done.far, bf16[1024,512]{1,0:T(8,128)(2,1)S(1)} %bitcast.5), custom_call_target="tpu_custom_call" | custom-call | tf_op jit(solution)/shard_map/cost/pallas_call | solution.py:299
  63.2 14.4 %all_to_all.51.refs_0_ = f32[32,8,128]{2,1,0:T(8,128)S(1)} all-to-all(f32[32,8,128]{2,1,0:T(8,128)S(1)} %broadcast_in_dim.23), channel_id=1, replica_groups=mesh['z'=8,'x'=4,'c'=2,'col'=8] {'z','x'}, dimensions={0} | all-to-all | bytes 262144 | tf_op jit(solution)/shard_map/all_to_all | solution.py:271
  77.6 4.0 %first_rows.1 = (f32[1024,1024]{1,0:T(8,128)S(1)}, f32[8,128]{1,0:T(8,128)S(1)}, f32[8,128]{1,0:T(8,128)S(1)}) custom-call(f32[32,8,128]{2,1,0:T(8,128)S(1)} %all_to_all.51.refs_0_, f32[1024,1024]{1,0:T(8,128)S(1)} %get-tuple-element.18.refs_1_), custom_call_target="tpu_custom_call" | custom-call | tf_op jit(solution)/shard_map/first_rows/pallas_call | solution.py:303
  81.6 15.2 %all_to_all.52.refs_0_ = f32[16,8,128]{2,1,0:T(8,128)S(1)} all-to-all(f32[16,8,128]{2,1,0:T(8,128)S(1)} %broadcast_in_dim.24), channel_id=1, replica_groups=mesh['z'=8,'x'=4,'c'=2,'col'=8] {'col','c'}, dimensions={0} | all-to-all | bytes 131072 | tf_op jit(solution)/shard_map/all_to_all | solution.py:271
  96.8 1.3 first_cols.1
  98.1 12.8 %all_to_all.53.refs_0_ = f32[32,8,128]{2,1,0:T(8,128)S(1)} all-to-all(f32[32,8,128]{2,1,0:T(8,128)S(1)} %broadcast_in_dim.25), channel_id=1, replica_groups=mesh['z'=8,'x'=4,'c'=2,'col'=8] {'z','x'}, dimensions={0} | all-to-all | bytes 262144 | tf_op jit(solution)/shard_map/all_to_all | solution.py:271
  110.9 0.7 rows.2
  111.7 11.8 %all_to_all.54.refs_0_ = f32[16,8,128]{2,1,0:T(8,128)S(1)} all-to-all(f32[16,8,128]{2,1,0:T(8,128)S(1)} %broadcast_in_dim.26), channel_id=1, replica_groups=mesh['z'=8,'x'=4,'c'=2,'col'=8] {'col','c'}, dimensions={0} | all-to-all | bytes 131072 | tf_op jit(solution)/shard_map/all_to_all | solution.py:271
  123.5 1.2 cols.2
  124.7 12.9 %all_to_all.55.refs_0_ = f32[32,8,128]{2,1,0:T(8,128)S(1)} all-to-all(f32[32,8,128]{2,1,0:T(8,128)S(1)} %broadcast_in_dim.27), channel_id=1, replica_groups=mesh['z'=8,'x'=4,'c'=2,'col'=8] {'z','x'}, dimensions={0} | all-to-all | bytes 262144 | tf_op jit(solution)/shard_map/all_to_all | solution.py:271
  137.6 0.7 rows.3
  138.4 11.8 %all_to_all.56.refs_0_ = f32[16,8,128]{2,1,0:T(8,128)S(1)} all-to-all(f32[16,8,128]{2,1,0:T(8,128)S(1)} %broadcast_in_dim.28), channel_id=1, replica_groups=mesh['z'=8,'x'=4,'c'=2,'col'=8] {'col','c'}, dimensions={0} | all-to-all | bytes 131072 | tf_op jit(solution)/shard_map/all_to_all | solution.py:271
  150.2 0.7 cols.3
  150.8 12.9 %all_to_all.57.refs_0_ = f32[32,8,128]{2,1,0:T(8,128)S(1)} all-to-all(f32[32,8,128]{2,1,0:T(8,128)S(1)} %broadcast_in_dim.29), channel_id=1, replica_groups=mesh['z'=8,'x'=4,'c'=2,'col'=8] {'z','x'}, dimensions={0} | all-to-all | bytes 262144 | tf_op jit(solution)/shard_map/all_to_all | solution.py:271
  163.7 1.4 targets_far.1
  165.1 3.5 %collective-permute-start.1 = (bf16[8,80,512]{2,1,0:T(8,128)(2,1)S(1)}, bf16[8,80,512]{2,1,0:T(8,128)(2,1)S(1)}, u32[]{:S(2)}, u32[]{:S(2)}) collective-permute-start(bf16[8,80,512]{2,1,0:T(8,128)(2,1)S(1)} %targets_far.1), channel_id=1, source_target_pairs={{0,8},{8,0},{1,9},{9,1},{2,10},{10,2},{3,11},{11,3},{4,12},{12,4},... | collective-permute-start | bytes 1966088 | tf_op jit(solution)/shard_map/ppermute | solution.py:275
  168.6 1.4 targets_own.1
  169.9 0.3 collective-permute-done.1.far
  170.3 0.2 pack.1
  170.4 23.2 %all_to_all.58.parts = bf16[8,80,512]{2,1,0:T(8,128)(2,1)S(1)} all-to-all(bf16[8,80,512]{2,1,0:T(8,128)(2,1)S(1)} %pack.1), channel_id=1, replica_groups=mesh['z'=8,'x'=4,'c'=2,'col'=8] {'col'}, dimensions={0} | all-to-all | bytes 1310720 | tf_op jit(solution)/shard_map/all_to_all | solution.py:335
  193.6 0.7 finish.1
  (7 shorter events, 0.1 us)
Async XLA Ops:
  0.0 26.9 %copy-start = (bf16[512,64]{0,1:T(8,128)(2,1)S(1)}, bf16[512,64]{0,1:T(8,128)(2,1)}, u32[]{:S(2)}) copy-start(bf16[512,64]{0,1:T(8,128)(2,1)} %param.2) | copy-start | bytes 196612
  22.9 37.5 %all-to-all-start.1 = ((bf16[4,256,512]{2,1,0:T(8,128)(2,1)}), bf16[4,256,512]{2,1,0:T(8,128)(2,1)S(1)}, u32[]{:S(2)}, u32[]{:S(2)}) async-start(bf16[4,256,512]{2,1,0:T(8,128)(2,1)} %broadcast_in_dim.22), calls=%async_computation.1 | async-start | bytes 2097152 | tf_op jit(solution)/shard_map/all_to_all | solution.py:271
  49.2 11.2 %collective-permute-start = (bf16[512,512]{1,0:T(8,128)(2,1)S(1)}, bf16[512,512]{1,0:T(8,128)(2,1)S(1)}, u32[]{:S(2)}, u32[]{:S(2)}) collective-permute-start(bf16[512,512]{1,0:T(8,128)(2,1)S(1)} %noise.1.own), channel_id=1, source_target_pairs={{0,8},{8,0},{1,9},{9,1},{2,10},{10,2},{3,11},{11,3},{4,12},{12,4},... | collective-permute-start | bytes 1572872 | tf_op jit(solution)/shard_map/ppermute | solution.py:275
  165.1 5.2 %collective-permute-start.1 = (bf16[8,80,512]{2,1,0:T(8,128)(2,1)S(1)}, bf16[8,80,512]{2,1,0:T(8,128)(2,1)S(1)}, u32[]{:S(2)}, u32[]{:S(2)}) collective-permute-start(bf16[8,80,512]{2,1,0:T(8,128)(2,1)S(1)} %targets_far.1), channel_id=1, source_target_pairs={{0,8},{8,0},{1,9},{9,1},{2,10},{10,2},{3,11},{11,3},{4,12},{12,4},... | collective-permute-start | bytes 1966088 | tf_op jit(solution)/shard_map/ppermute | solution.py:275

commit v2 on v1

--- a/solution.py
+++ b/solution.py
@@ -265,10 +265,24 @@
     out[...] = (total / add_three(functools.reduce(jnp.add, tails))).astype(BF16)
 
 
+def join_body(how, parts, out):
+    out[...] = how([parts])
+
+
 def everyone(val, axes):
     count = lax.axis_size(axes)
     copies = jnp.broadcast_to(val[None], (count,) + val.shape)
     return lax.all_to_all(copies, axes, 0, 0, tiled=True)
+
+
+def joined(how, val):
+    return call(functools.partial(join_body, how), jax.ShapeDtypeStruct(val.shape[1:], F32), 1, name="join")(val)
+
+
+def by_axis(how, val, axes):
+    for axis in axes[:-1]:
+        val = joined(how, lax.all_gather(val, axis, axis=0))
+    return lax.all_gather(val, axes[-1], axis=0)
 
 
 def swapped(val):
@@ -286,8 +300,7 @@
     row_axes, col_axes = ("z", "x"), ("col", "c")
 
     noise_parts = lax.all_gather(noise.T, "col", axis=0)
-    stacked = everyone(data, "z").reshape(data.shape[0] * zs, depth)
-    data_all = everyone(stacked, "x").reshape(wide, depth)
+    data_all = everyone(data, ("z", "x")).reshape(wide, depth)
     own = call(noise_body, jax.ShapeDtypeStruct((half, depth), BF16), 1, name="noise")(noise_parts)
     far = swapped(own)
 
@@ -299,22 +312,22 @@
     score, lse = call(
         cost_body, (tile, vec_col), 3, [pltpu.VMEM((cs, half, 128), F32)], name="cost"
     )(own, far, data_all)
-    parts = everyone(lse, row_axes)
+    parts = by_axis(merged, lse, ("z", "x"))
     expd, peak, lse = call(
         functools.partial(first_row_body, log_data, 1),
         (tile, vec_row, vec_row), 2, [strip, strip], name="first_rows",
     )(parts, score)
-    parts = everyone(lse, col_axes)
+    parts = by_axis(merged, lse, ("c", "col"))
     sums, scale, factor = call(
         functools.partial(first_col_body, count_noise, 1),
         (vec_col, vec_row, vec_row), 3, [strip], name="first_cols",
     )(parts, peak, expd)
     for sweep in range(1, ITERS - 1):
-        parts = everyone(sums, row_axes)
+        parts = by_axis(added, sums, ("x", "z")) if sweep == 2 else everyone(sums, row_axes)
         mass = call(
             functools.partial(row_body, count_data, 1), vec_row, 3, [strip], name="rows"
         )(parts, scale, expd)
-        parts = everyone(mass, col_axes)
+        parts = by_axis(added, mass, ("col", "c")) if sweep == 2 else everyone(mass, col_axes)
         sums, factor = call(
             functools.partial(col_body, count_noise, 1), (vec_col, vec_row), 3, [strip], name="cols"
         )(parts, scale, expd)

time: 195 us -> 261 us (1.34)
  blocking collectives: 158 us -> 216 us
  starting transfers between devices: 17.2 us -> 25.4 us
    all_gather x0 -> x8, blocking collectives: none -> 120 us  [the longest x4 62.8 us: by_axis(): return lax.all_gather(val, axes[-1], axis=0)]
    all_to_all x8 -> x3, blocking collectives: 113 us -> 51.5 us  [everyone(): return lax.all_to_all(copies, axes, 0, 0, tiled=True)]
    all_to_all x1, starting transfers between devices: 4.01 us -> 13.7 us  [everyone(): return lax.all_to_all(copies, axes, 0, 0, tiled=True)]
where the time goes in v2:
time: 261 us
  blocking collectives  216 us (83%)
  starting transfers between devices  25.4 us (10%)
  Pallas kernels  15.4 us (6%)
    all_gather x4, blocking collectives, by_axis(): return lax.all_gather(val, axes[-1], axis=0)  62.8 us
    all_gather x4, blocking collectives, by_axis(): val = joined(how, lax.all_gather(val, axis, axis=0))  57.6 us
    all_to_all x3, blocking collectives, everyone(): return lax.all_to_all(copies, axes, 0, 0, tiled=True)  51.5 us
    all_gather x1, blocking collectives, on_device(): noise_parts = lax.all_gather(noise.T, 'col', axis=0)  22.4 us
    all_to_all x1, blocking collectives, on_device(): got = lax.all_to_all(pieces, 'col', 0, 0, tiled=True)  21.9 us
    all_to_all x1, starting transfers between devices, everyone(): return lax.all_to_all(copies, axes, 0, 0, tiled=True)  13.7 us
    ppermute x2, starting transfers between devices, swapped(): return lax.ppermute(val, 'c', [(0, 1), (1, 0)])  11.7 us
  transfers between devices with their start and end apart: 3, of which 2 were waited for; matrix products, arithmetic and copies ran while one was open for 0% of the time, Pallas kernels for 1%

profile of v2, /device:TPU:1, one launch (start us, length us, event | category | flops | bytes accessed | tf_op | source)
XLA Modules:
  0.0 260.8 jit_solution(11233297064402093481)
XLA Ops:
  0.0 1.8 broadcast_in_dim.8
  1.8 13.7 %all-to-all-start = ((bf16[32,32,512]{2,1,0:T(8,128)(2,1)}), bf16[32,32,512]{2,1,0:T(8,128)(2,1)S(1)}, u32[]{:S(2)}, u32[]{:S(2)}) async-start(bf16[32,32,512]{2,1,0:T(8,128)(2,1)} %broadcast_in_dim.8), calls=%async_computation | async-start | bytes 2097152 | tf_op jit(solution)/shard_map/all_to_all | solution.py:275
  15.6 22.4 %all-gather = bf16[512,512]{1,0:T(8,128)(2,1)S(1)} all-gather(bf16[64,512]{1,0:T(8,128)(2,1)} %bitcast.24), channel_id=2, replica_groups=mesh['z'=8,'x'=4,'c'=2,'col'=8] {'col'}, dimensions={0}, use_global_device_ids=true | all-gather | bytes 589824 | tf_op jit(solution)/shard_map/all_gather | solution.py:302
  38.0 0.5 noise.1.own
  38.5 7.8 %collective-permute-start = (bf16[512,512]{1,0:T(8,128)(2,1)S(1)}, bf16[512,512]{1,0:T(8,128)(2,1)S(1)}, u32[]{:S(2)}, u32[]{:S(2)}) collective-permute-start(bf16[512,512]{1,0:T(8,128)(2,1)S(1)} %noise.1.own), channel_id=1, source_target_pairs={{0,8},{8,0},{1,9},{9,1},{2,10},{10,2},{3,11},{11,3},{4,12},{12,4},... | collective-permute-start | bytes 1572872 | tf_op jit(solution)/shard_map/ppermute | solution.py:289
  46.2 1.5 collective-permute-done.far
  47.8 0.0 all-to-all-done
  47.8 2.7 %cost.1 = (f32[1024,1024]{1,0:T(8,128)S(1)}, f32[8,128]{1,0:T(8,128)S(1)}) custom-call(bf16[512,512]{1,0:T(8,128)(2,1)S(1)} %noise.1.own, bf16[512,512]{1,0:T(8,128)(2,1)S(1)} %collective-permute-done.far, bf16[1024,512]{1,0:T(8,128)(2,1)S(1)} %bitcast.12), custom_call_target="tpu_custom_call" | custom-call | tf_op jit(solution)/shard_map/cost/pallas_call | solution.py:312
  50.5 19.3 %all-gather.1 = f32[64,128]{1,0:T(8,128)S(1)} all-gather(f32[8,128]{1,0:T(8,128)S(1)} %get-tuple-element.17), channel_id=3, replica_groups=mesh['z'=8,'x'=4,'c'=2,'col'=8] {'z'}, dimensions={0}, use_global_device_ids=true | all-gather | bytes 36864 | tf_op jit(solution)/shard_map/all_gather | solution.py:284
  69.9 9.3 %all-gather.2 = f32[32,128]{1,0:T(8,128)S(1)} all-gather(f32[8,128]{1,0:T(8,128)S(1)} %join.4), channel_id=4, replica_groups=mesh['z'=8,'x'=4,'c'=2,'col'=8] {'x'}, dimensions={0}, use_global_device_ids=true | all-gather | bytes 20480 | tf_op jit(solution)/shard_map/all_gather | solution.py:285
  79.2 3.9 %first_rows.1 = (f32[1024,1024]{1,0:T(8,128)S(1)}, f32[8,128]{1,0:T(8,128)S(1)}, f32[8,128]{1,0:T(8,128)S(1)}) custom-call(f32[4,8,128]{2,1,0:T(8,128)S(1)} %bitcast.20, f32[1024,1024]{1,0:T(8,128)S(1)} %get-tuple-element.18.refs_1_), custom_call_target="tpu_custom_call" | custom-call | tf_op jit(solution)/shard_map/first_rows/pallas_call | solution.py:316
  83.1 11.1 %all-gather.3 = f32[16,128]{1,0:T(8,128)S(1)} all-gather(f32[8,128]{1,0:T(8,128)S(1)} %get-tuple-element.19), channel_id=5, replica_groups=mesh['z'=8,'x'=4,'c'=2,'col'=8] {'c'}, dimensions={0}, use_global_device_ids=true | all-gather | bytes 12288 | tf_op jit(solution)/shard_map/all_gather | solution.py:284
  94.3 18.1 %all-gather.4 = f32[64,128]{1,0:T(8,128)S(1)} all-gather(f32[8,128]{1,0:T(8,128)S(1)} %join.5), channel_id=6, replica_groups=mesh['z'=8,'x'=4,'c'=2,'col'=8] {'col'}, dimensions={0}, use_global_device_ids=true | all-gather | bytes 36864 | tf_op jit(solution)/shard_map/all_gather | solution.py:285
  112.4 1.3 first_cols.1
  113.6 16.8 %all_to_all.25.refs_0_ = f32[32,8,128]{2,1,0:T(8,128)S(1)} all-to-all(f32[32,8,128]{2,1,0:T(8,128)S(1)} %broadcast_in_dim.9), channel_id=1, replica_groups=mesh['z'=8,'x'=4,'c'=2,'col'=8] {'z','x'}, dimensions={0} | all-to-all | bytes 262144 | tf_op jit(solution)/shard_map/all_to_all | solution.py:275
  130.4 0.7 rows.2
  131.2 21.3 %all_to_all.26.refs_0_ = f32[16,8,128]{2,1,0:T(8,128)S(1)} all-to-all(f32[16,8,128]{2,1,0:T(8,128)S(1)} %broadcast_in_dim.10), channel_id=1, replica_groups=mesh['z'=8,'x'=4,'c'=2,'col'=8] {'col','c'}, dimensions={0} | all-to-all | bytes 131072 | tf_op jit(solution)/shard_map/all_to_all | solution.py:275
  152.5 1.2 cols.2
  153.7 9.0 %all-gather.5 = f32[32,128]{1,0:T(8,128)S(1)} all-gather(f32[8,128]{1,0:T(8,128)S(1)} %get-tuple-element.24), channel_id=7, replica_groups=mesh['z'=8,'x'=4,'c'=2,'col'=8] {'x'}, dimensions={0}, use_global_device_ids=true | all-gather | bytes 20480 | tf_op jit(solution)/shard_map/all_gather | solution.py:284
  162.7 18.1 %all-gather.6 = f32[64,128]{1,0:T(8,128)S(1)} all-gather(f32[8,128]{1,0:T(8,128)S(1)} %join.6), channel_id=8, replica_groups=mesh['z'=8,'x'=4,'c'=2,'col'=8] {'z'}, dimensions={0}, use_global_device_ids=true | all-gather | bytes 36864 | tf_op jit(solution)/shard_map/all_gather | solution.py:285
  180.8 0.7 rows.3
  181.6 18.1 %all-gather.7 = f32[64,128]{1,0:T(8,128)S(1)} all-gather(f32[8,128]{1,0:T(8,128)S(1)} %rows.3), channel_id=9, replica_groups=mesh['z'=8,'x'=4,'c'=2,'col'=8] {'col'}, dimensions={0}, use_global_device_ids=true | all-gather | bytes 36864 | tf_op jit(solution)/shard_map/all_gather | solution.py:284
  199.7 17.3 %all-gather.8 = f32[16,128]{1,0:T(8,128)S(1)} all-gather(f32[8,128]{1,0:T(8,128)S(1)} %join.7), channel_id=10, replica_groups=mesh['z'=8,'x'=4,'c'=2,'col'=8] {'c'}, dimensions={0}, use_global_device_ids=true | all-gather | bytes 12288 | tf_op jit(solution)/shard_map/all_gather | solution.py:285
  216.9 0.6 cols.3
  217.6 13.4 %all_to_all.27.refs_0_ = f32[32,8,128]{2,1,0:T(8,128)S(1)} all-to-all(f32[32,8,128]{2,1,0:T(8,128)S(1)} %broadcast_in_dim.11), channel_id=1, replica_groups=mesh['z'=8,'x'=4,'c'=2,'col'=8] {'z','x'}, dimensions={0} | all-to-all | bytes 262144 | tf_op jit(solution)/shard_map/all_to_all | solution.py:275
  231.0 1.3 targets_far.1
  232.3 3.9 %collective-permute-start.1 = (bf16[8,80,512]{2,1,0:T(8,128)(2,1)S(1)}, bf16[8,80,512]{2,1,0:T(8,128)(2,1)S(1)}, u32[]{:S(2)}, u32[]{:S(2)}) collective-permute-start(bf16[8,80,512]{2,1,0:T(8,128)(2,1)S(1)} %targets_far.1), channel_id=1, source_target_pairs={{0,8},{8,0},{1,9},{9,1},{2,10},{10,2},{3,11},{11,3},{4,12},{12,4},... | collective-permute-start | bytes 1966088 | tf_op jit(solution)/shard_map/ppermute | solution.py:289
  236.3 1.4 targets_own.1
  237.7 0.3 collective-permute-done.1.far
  238.0 0.2 pack.1
  238.1 21.9 %all_to_all.28.parts = bf16[8,80,512]{2,1,0:T(8,128)(2,1)S(1)} all-to-all(bf16[8,80,512]{2,1,0:T(8,128)(2,1)S(1)} %pack.1), channel_id=1, replica_groups=mesh['z'=8,'x'=4,'c'=2,'col'=8] {'col'}, dimensions={0} | all-to-all | bytes 1310720 | tf_op jit(solution)/shard_map/all_to_all | solution.py:348
  260.1 0.7 finish.1
  (7 shorter events, 0.1 us)
Async XLA Ops:
  1.8 45.9 %all-to-all-start = ((bf16[32,32,512]{2,1,0:T(8,128)(2,1)}), bf16[32,32,512]{2,1,0:T(8,128)(2,1)S(1)}, u32[]{:S(2)}, u32[]{:S(2)}) async-start(bf16[32,32,512]{2,1,0:T(8,128)(2,1)} %broadcast_in_dim.8), calls=%async_computation | async-start | bytes 2097152 | tf_op jit(solution)/shard_map/all_to_all | solution.py:275
  38.5 9.3 %collective-permute-start = (bf16[512,512]{1,0:T(8,128)(2,1)S(1)}, bf16[512,512]{1,0:T(8,128)(2,1)S(1)}, u32[]{:S(2)}, u32[]{:S(2)}) collective-permute-start(bf16[512,512]{1,0:T(8,128)(2,1)S(1)} %noise.1.own), channel_id=1, source_target_pairs={{0,8},{8,0},{1,9},{9,1},{2,10},{10,2},{3,11},{11,3},{4,12},{12,4},... | collective-permute-start | bytes 1572872 | tf_op jit(solution)/shard_map/ppermute | solution.py:289
  232.3 5.6 %collective-permute-start.1 = (bf16[8,80,512]{2,1,0:T(8,128)(2,1)S(1)}, bf16[8,80,512]{2,1,0:T(8,128)(2,1)S(1)}, u32[]{:S(2)}, u32[]{:S(2)}) collective-permute-start(bf16[8,80,512]{2,1,0:T(8,128)(2,1)S(1)} %targets_far.1), channel_id=1, source_target_pairs={{0,8},{8,0},{1,9},{9,1},{2,10},{10,2},{3,11},{11,3},{4,12},{12,4},... | collective-permute-start | bytes 1966088 | tf_op jit(solution)/shard_map/ppermute | solution.py:289

commit v3 on v1

--- a/solution.py
+++ b/solution.py
@@ -81,77 +81,82 @@
     return functools.reduce(jnp.add, parts_of(refs))
 
 
-def noise_body(parts, out):
-    for r in range(out.shape[0] // 128):
-        at = slice(r * 128, (r + 1) * 128)
-        block = jnp.concatenate(
-            [parts[k, :, at].astype(F32).T for k in range(parts.shape[0])], axis=1
-        )
-        out[at, :] = block.astype(BF16)
-
-
-def half_at(flip, rows):
-    return pl.multiple_of(lax.rem(lax.axis_index("c") + flip, 2) * rows, rows)
-
-
-def cost_body(own, far, data, score, lse, sq):
-    rows, depth = own.shape
-    width = 256
-    ones = jnp.ones((8, depth), BF16)
+def noise_body(parts, out, sq):
+    cols, cores, depth, half = parts.shape
+    for c in range(cores):
+        for r in range(half // 128):
+            at = slice(r * 128, (r + 1) * 128)
+            total = jnp.zeros((1, 128), F32)
+            blocks = []
+            for k in range(cols):
+                block = parts[k, c, :, at].astype(F32)
+                total = total + jnp.sum(block * block, axis=0, keepdims=True)
+                blocks.append(block.T)
+            row = c * (half // 128) + r
+            out[row * 128 : (row + 1) * 128, :] = jnp.concatenate(blocks, axis=1).astype(BF16)
+            sq[row : row + 1, :] = total
+
+
+def cost_body(noise, noise_sq, data, score, lse, rows_sq, part):
+    rows, depth = noise.shape
+    width, step = 256, min(rows, 512)
     contract = (((1,), (1,)), ((), ()))
-    for flip, noise in enumerate((own, far)):
-        for r in range(rows // 128):
-            block = noise[r * 128 : (r + 1) * 128, :].astype(F32)
-            total = jnp.sum(lane_sum(block * block), axis=1, keepdims=True)
-            sq[flip, r * 128 : (r + 1) * 128, :] = jnp.broadcast_to(total, (128, 128))
+    lanes_to_rows(noise_sq[...], rows_sq)
     for b in range(data.shape[0] // width):
         at = slice(b * width, (b + 1) * width)
         piece = data[at, :]
         wide = piece.astype(F32)
-        square = wide * wide
-        high = square.astype(BF16)
-        low = (square - high.astype(F32)).astype(BF16)
-        piece_sq = lax.dot_general(ones, high, contract, preferred_element_type=F32)
-        piece_sq += lax.dot_general(ones, low, contract, preferred_element_type=F32)
-        vals, tops = [], []
-        for flip, noise in enumerate((own, far)):
-            cross = lax.dot_general(noise[...], piece, contract, preferred_element_type=F32)
-            rows_sq = jnp.concatenate([sq[flip]] * (width // 128), axis=1)
-            val = (2.0 * cross - rows_sq - piece_sq[0:1, :]) * (1.0 / (depth * EPS))
-            score[pl.ds(half_at(flip, rows), rows), at] = val
-            vals.append(val)
+        part[at, :] = lane_sum(wide * wide)
+        piece_sq = flat(rows_to_lanes(part.at[at, :]))
+        tops = []
+        for r in range(rows // step):
+            here = slice(r * step, (r + 1) * step)
+            cross = lax.dot_general(noise[here, :], piece, contract, preferred_element_type=F32)
+            sq = jnp.concatenate([rows_sq[here, :]] * (width // 128), axis=1)
+            val = (2.0 * cross - sq - piece_sq) * (1.0 / (depth * EPS))
+            score[here, at] = val
             tops.append(jnp.max(val, axis=0, keepdims=True))
-        top = jnp.maximum(tops[0], tops[1])
-        total = sum(jnp.sum(jnp.exp(val - top), axis=0, keepdims=True) for val in vals)
-        part = top + jnp.log(total)
+        top = functools.reduce(jnp.maximum, tops)
+        total = jnp.sum(jnp.exp(score[:, at] - top), axis=0, keepdims=True)
+        sums = top + jnp.log(total)
         for t in range(width // 128):
             row = b * (width // 128) + t
-            lse[row : row + 1, :] = part[:, t * 128 : (t + 1) * 128]
+            lse[row : row + 1, :] = sums[:, t * 128 : (t + 1) * 128]
 
 
 def first_row_body(log_data, n, *refs):
     parts, (score, expd, peak, lse, part, tops) = refs[:n], refs[n:]
-    pot = flat(-log_data - merged(parts))
-    rows = expd.shape[0]
-    step = 32
-
-    def body(r, carry):
-        at = pl.ds(pl.multiple_of(r * step, step), step)
+    rows, cols = expd.shape
+    pot = jnp.broadcast_to(flat(-log_data - merged(parts)), (8, cols))
+
+    def find(r, carry):
+        at = pl.ds(pl.multiple_of(r * 8, 8), 8)
         val = score[at, :] + pot
-        top = jnp.max(val, axis=1, keepdims=True)
-        e = jnp.exp(val - (top - SHIFT))
+        part[at, :] = functools.reduce(
+            jnp.maximum, [val[:, t * 128 : (t + 1) * 128] for t in range(cols // 128)]
+        )
+        return carry
+
+    lax.fori_loop(0, rows // 8, find, 0, unroll=8)
+    high = jnp.concatenate(
+        [
+            jnp.max(part[r * 128 : (r + 1) * 128, :].T, axis=0, keepdims=True)
+            for r in range(rows // 128)
+        ],
+        axis=0,
+    )
+    lanes_to_rows(high - SHIFT, tops)
+
+    def raise_up(r, carry):
+        at = pl.ds(pl.multiple_of(r * 8, 8), 8)
+        e = jnp.exp((score[at, :] + pot) - jnp.concatenate([tops[at, :]] * (cols // 128), axis=1))
         expd[at, :] = e
         part[at, :] = lane_sum(e)
-        tops[at, :] = jnp.broadcast_to(top, (step, 128))
         return carry
 
-    lax.fori_loop(0, rows // step, body, 0)
-    sums = rows_to_lanes(part)
-    high = jnp.concatenate(
-        [tops[r * 128 : (r + 1) * 128, :].T[0:1, :] for r in range(rows // 128)], axis=0
-    )
+    lax.fori_loop(0, rows // 8, raise_up, 0, unroll=8)
     peak[...] = high
-    lse[...] = high + (jnp.log(sums) - SHIFT)
+    lse[...] = high + (jnp.log(rows_to_lanes(part)) - SHIFT)
 
 
 def column_sums(expd, factor, factors, out):
@@ -164,7 +169,7 @@
         f = factors[at, :]
         return acc + expd[at, :] * jnp.concatenate([f] * copies, axis=1)
 
-    acc = lax.fori_loop(0, rows // 8, body, jnp.zeros((8, cols), F32), unroll=4)
+    acc = lax.fori_loop(0, rows // 8, body, jnp.zeros((8, cols), F32), unroll=8)
     sums = jnp.sum(acc, axis=0, keepdims=True)
     count, width = out.shape
     for t in range(count):
@@ -172,19 +177,17 @@
 
 
 def first_col_body(count, n, *refs):
-    parts, (peak, expd, out, scale, factor, factors) = refs[:n], refs[n:]
-    lse = merged(parts)
-    s = jnp.exp(peak[...] - lse + SHIFT)
+    parts, (peak, expd, out, scale, factors) = refs[:n], refs[n:]
+    s = jnp.exp(peak[...] - merged(parts) + SHIFT)
     scale[...] = s
-    f = s * (1.0 / count)
-    factor[...] = f
-    column_sums(expd, f, factors, out)
+    column_sums(expd, s * (1.0 / count), factors, out)
 
 
 def col_body(count, n, *refs):
-    parts, (scale, expd, out, factor, factors) = refs[:n], refs[n:]
+    parts, (scale, expd, out, *factor, factors) = refs[:n], refs[n:]
     f = scale[...] * ((SCALE / count) / added(parts))
-    factor[...] = f
+    for ref in factor:
+        ref[...] = f
     column_sums(expd, f, factors, out)
 
 
@@ -198,8 +201,12 @@
         part[at, :] = lane_sum(expd[at, :] * v)
         return carry
 
-    lax.fori_loop(0, rows // 8, body, 0, unroll=4)
+    lax.fori_loop(0, rows // 8, body, 0, unroll=8)
     out[...] = rows_to_lanes(part) * scale[...]
+
+
+def half_at(flip, rows):
+    return pl.multiple_of(lax.rem(lax.axis_index("c") + flip, 2) * rows, rows)
 
 
 def split_three(mass, deep):
@@ -285,29 +292,30 @@
     log_data = math.log(count_data)
     row_axes, col_axes = ("z", "x"), ("col", "c")
 
-    noise_parts = lax.all_gather(noise.T, "col", axis=0)
-    stacked = everyone(data, "z").reshape(data.shape[0] * zs, depth)
-    data_all = everyone(stacked, "x").reshape(wide, depth)
-    own = call(noise_body, jax.ShapeDtypeStruct((half, depth), BF16), 1, name="noise")(noise_parts)
-    far = swapped(own)
+    noise_parts = lax.all_gather(noise.T, ("col", "c"), axis=0)
+    noise_parts = noise_parts.reshape(cols_all, cs, slice_width, half)
+    data_all = everyone(data, ("z", "x")).reshape(wide, depth)
 
     vec_col = jax.ShapeDtypeStruct((wide // 128, 128), F32)
     vec_row = jax.ShapeDtypeStruct((rows // 128, 128), F32)
     tile = vmem((rows, wide), F32)
     strip = pltpu.VMEM((rows, 128), F32)
 
+    noise_all, noise_sq = call(
+        noise_body, (jax.ShapeDtypeStruct((rows, depth), BF16), vec_row), 1, name="noise"
+    )(noise_parts)
     score, lse = call(
-        cost_body, (tile, vec_col), 3, [pltpu.VMEM((cs, half, 128), F32)], name="cost"
-    )(own, far, data_all)
+        cost_body, (tile, vec_col), 3, [strip, pltpu.VMEM((wide, 128), F32)], name="cost"
+    )(noise_all, noise_sq, data_all)
     parts = everyone(lse, row_axes)
     expd, peak, lse = call(
         functools.partial(first_row_body, log_data, 1),
         (tile, vec_row, vec_row), 2, [strip, strip], name="first_rows",
     )(parts, score)
     parts = everyone(lse, col_axes)
-    sums, scale, factor = call(
+    sums, scale = call(
         functools.partial(first_col_body, count_noise, 1),
-        (vec_col, vec_row, vec_row), 3, [strip], name="first_cols",
+        (vec_col, vec_row), 3, [strip], name="first_cols",
     )(parts, peak, expd)
     for sweep in range(1, ITERS - 1):
         parts = everyone(sums, row_axes)
@@ -315,9 +323,12 @@
             functools.partial(row_body, count_data, 1), vec_row, 3, [strip], name="rows"
         )(parts, scale, expd)
         parts = everyone(mass, col_axes)
-        sums, factor = call(
-            functools.partial(col_body, count_noise, 1), (vec_col, vec_row), 3, [strip], name="cols"
+        last = sweep == ITERS - 2
+        sums, *factor = call(
+            functools.partial(col_body, count_noise, 1),
+            (vec_col, vec_row) if last else (vec_col,), 3, [strip], name="cols",
         )(parts, scale, expd)
+    (factor,) = factor
     parts = everyone(sums, row_axes)
 
     strips = [pltpu.VMEM((half, 128), F32)] * 2 + [pltpu.VMEM((half, wide), BF16)]

time: 195 us -> 211 us (1.082)
  waiting for transfers between devices: 1.85 us -> 46.1 us
  blocking collectives: 158 us -> 119 us
  between operations: 0.12 us -> 13.5 us
  Pallas kernels: 15.4 us -> 11.7 us
    all_gather x0 -> x1, waiting for transfers between devices: none -> 45.1 us  [on_device(): noise_parts = lax.all_gather(noise.T, ('col', 'c'), axis=0)]
    all_gather x1 -> x0, blocking collectives: 21.8 us -> none  [on_device(): noise_parts = lax.all_gather(noise.T, 'col', axis=0)]
    all_to_all x8 -> x7, blocking collectives: 113 us -> 95.4 us  [everyone(): return lax.all_to_all(copies, axes, 0, 0, tiled=True)]
    all_to_all x1, starting transfers between devices: 4.01 us -> 13.7 us  [everyone(): return lax.all_to_all(copies, axes, 0, 0, tiled=True)]
    ppermute x2 -> x1, starting transfers between devices: 13.1 us -> 3.47 us  [swapped(): return lax.ppermute(val, 'c', [(0, 1), (1, 0)])]
where the time goes in v3:
time: 211 us; the launch traced here: 210 us
  blocking collectives  119 us (56%)
  waiting for transfers between devices  46.1 us (22%)
  starting transfers between devices  17.2 us (8%)
  between operations  13.5 us (6%)
  Pallas kernels  11.7 us (6%)
  local copies, waits for them, and re-layouts  3.14 us (1%)
    all_to_all x7, blocking collectives, everyone(): return lax.all_to_all(copies, axes, 0, 0, tiled=True)  95.4 us
    all_gather x1, waiting for transfers between devices, on_device(): noise_parts = lax.all_gather(noise.T, ('col', 'c'), axis=0)  45.1 us
    all_to_all x1, blocking collectives, on_device(): got = lax.all_to_all(pieces, 'col', 0, 0, tiled=True)  23.2 us
    all_to_all x1, starting transfers between devices, everyone(): return lax.all_to_all(copies, axes, 0, 0, tiled=True)  13.7 us
  transfers between devices with their start and end apart: 3, of which 2 were waited for; matrix products, arithmetic and copies ran while one was open for 0% of the time, Pallas kernels for 1%

profile of v3, /device:TPU:1, one launch (start us, length us, event | category | flops | bytes accessed | tf_op | source)
XLA Modules:
  0.0 210.3 jit_solution(3400613191144045560)
XLA Ops:
  6.5 1.8 broadcast_in_dim.16
  8.4 13.7 %all-to-all-start = ((bf16[32,32,512]{2,1,0:T(8,128)(2,1)}), bf16[32,32,512]{2,1,0:T(8,128)(2,1)S(1)}, u32[]{:S(2)}, u32[]{:S(2)}) async-start(bf16[32,32,512]{2,1,0:T(8,128)(2,1)} %broadcast_in_dim.16), calls=%async_computation | async-start | bytes 2097152 | tf_op jit(solution)/shard_map/all_to_all | solution.py:278
  22.1 0.0 all-gather.3.cloned.1.call-start
  22.2 0.7 all-gather.3.cloned.1.call-update
  22.8 45.1 %all-gather.3.cloned.1.call-done = bf16[1024,512]{1,0:T(8,128)(2,1)} async-done(((bf16[64,512]{1,0:T(8,128)(2,1)}), bf16[1024,512]{1,0:T(8,128)(2,1)}) %all-gather.3.cloned.1.call-update) | async-done | bytes 1048592 | tf_op jit(solution)/shard_map/all_gather | solution.py:295
  67.9 0.0 copy-start
  67.9 1.2 copy-done
  69.1 0.9 noise.1
  70.1 0.0 all-to-all-done
  70.1 2.1 cost.1
  72.2 19.2 %all_to_all.45.refs_0_ = f32[32,8,128]{2,1,0:T(8,128)S(1)} all-to-all(f32[32,8,128]{2,1,0:T(8,128)S(1)} %broadcast_in_dim.17), channel_id=1, replica_groups=mesh['z'=8,'x'=4,'c'=2,'col'=8] {'z','x'}, dimensions={0} | all-to-all | bytes 262144 | tf_op jit(solution)/shard_map/all_to_all | solution.py:278
  91.4 2.1 first_rows.1
  93.5 14.0 %all_to_all.46.refs_0_ = f32[16,8,128]{2,1,0:T(8,128)S(1)} all-to-all(f32[16,8,128]{2,1,0:T(8,128)S(1)} %broadcast_in_dim.18), channel_id=1, replica_groups=mesh['z'=8,'x'=4,'c'=2,'col'=8] {'col','c'}, dimensions={0} | all-to-all | bytes 131072 | tf_op jit(solution)/shard_map/all_to_all | solution.py:278
  107.5 0.6 first_cols.1
  108.1 12.9 %all_to_all.47.refs_0_ = f32[32,8,128]{2,1,0:T(8,128)S(1)} all-to-all(f32[32,8,128]{2,1,0:T(8,128)S(1)} %broadcast_in_dim.19), channel_id=1, replica_groups=mesh['z'=8,'x'=4,'c'=2,'col'=8] {'z','x'}, dimensions={0} | all-to-all | bytes 262144 | tf_op jit(solution)/shard_map/all_to_all | solution.py:278
  121.0 0.6 rows.2
  121.6 11.8 %all_to_all.48.refs_0_ = f32[16,8,128]{2,1,0:T(8,128)S(1)} all-to-all(f32[16,8,128]{2,1,0:T(8,128)S(1)} %broadcast_in_dim.20), channel_id=1, replica_groups=mesh['z'=8,'x'=4,'c'=2,'col'=8] {'col','c'}, dimensions={0} | all-to-all | bytes 131072 | tf_op jit(solution)/shard_map/all_to_all | solution.py:278
  133.4 0.6 cols.2
  134.0 12.9 %all_to_all.49.refs_0_ = f32[32,8,128]{2,1,0:T(8,128)S(1)} all-to-all(f32[32,8,128]{2,1,0:T(8,128)S(1)} %broadcast_in_dim.21), channel_id=1, replica_groups=mesh['z'=8,'x'=4,'c'=2,'col'=8] {'z','x'}, dimensions={0} | all-to-all | bytes 262144 | tf_op jit(solution)/shard_map/all_to_all | solution.py:278
  146.9 0.6 rows.3
  147.6 11.8 %all_to_all.50.refs_0_ = f32[16,8,128]{2,1,0:T(8,128)S(1)} all-to-all(f32[16,8,128]{2,1,0:T(8,128)S(1)} %broadcast_in_dim.22), channel_id=1, replica_groups=mesh['z'=8,'x'=4,'c'=2,'col'=8] {'col','c'}, dimensions={0} | all-to-all | bytes 131072 | tf_op jit(solution)/shard_map/all_to_all | solution.py:278
  159.4 0.6 cols.3
  160.0 12.9 %all_to_all.51.refs_0_ = f32[32,8,128]{2,1,0:T(8,128)S(1)} all-to-all(f32[32,8,128]{2,1,0:T(8,128)S(1)} %broadcast_in_dim.23), channel_id=1, replica_groups=mesh['z'=8,'x'=4,'c'=2,'col'=8] {'z','x'}, dimensions={0} | all-to-all | bytes 262144 | tf_op jit(solution)/shard_map/all_to_all | solution.py:278
  172.9 1.4 targets_far.1
  174.2 3.5 %collective-permute-start = (bf16[8,80,512]{2,1,0:T(8,128)(2,1)S(1)}, bf16[8,80,512]{2,1,0:T(8,128)(2,1)S(1)}, u32[]{:S(2)}, u32[]{:S(2)}) collective-permute-start(bf16[8,80,512]{2,1,0:T(8,128)(2,1)S(1)} %targets_far.1), channel_id=1, source_target_pairs={{0,8},{8,0},{1,9},{9,1},{2,10},{10,2},{3,11},{11,3},{4,12},{12,4},... | collective-permute-start | bytes 1966088 | tf_op jit(solution)/shard_map/ppermute | solution.py:282
  177.7 1.4 targets_own.1
  179.1 0.3 collective-permute-done.far
  179.4 0.2 pack.1
  179.6 23.2 %all_to_all.52.parts = bf16[8,80,512]{2,1,0:T(8,128)(2,1)S(1)} all-to-all(bf16[8,80,512]{2,1,0:T(8,128)(2,1)S(1)} %pack.1), channel_id=1, replica_groups=mesh['z'=8,'x'=4,'c'=2,'col'=8] {'col'}, dimensions={0} | all-to-all | bytes 1310720 | tf_op jit(solution)/shard_map/all_to_all | solution.py:346
  202.7 0.7 finish.1
  (7 shorter events, 0.1 us)
Async XLA Ops:
  8.4 61.7 %all-to-all-start = ((bf16[32,32,512]{2,1,0:T(8,128)(2,1)}), bf16[32,32,512]{2,1,0:T(8,128)(2,1)S(1)}, u32[]{:S(2)}, u32[]{:S(2)}) async-start(bf16[32,32,512]{2,1,0:T(8,128)(2,1)} %broadcast_in_dim.16), calls=%async_computation | async-start | bytes 2097152 | tf_op jit(solution)/shard_map/all_to_all | solution.py:278
  22.1 45.8 %all-gather.3.cloned.1.call-start = ((), (), s32[]{:S(2)}) async-start(), calls=%async_computation.9 | async-start | bytes 1114112 | tf_op jit(solution)/shard_map/all_gather | solution.py:295
  67.9 1.2 copy-start
  174.2 5.2 %collective-permute-start = (bf16[8,80,512]{2,1,0:T(8,128)(2,1)S(1)}, bf16[8,80,512]{2,1,0:T(8,128)(2,1)S(1)}, u32[]{:S(2)}, u32[]{:S(2)}) collective-permute-start(bf16[8,80,512]{2,1,0:T(8,128)(2,1)S(1)} %targets_far.1), channel_id=1, source_target_pairs={{0,8},{8,0},{1,9},{9,1},{2,10},{10,2},{3,11},{11,3},{4,12},{12,4},... | collective-permute-start | bytes 1966088 | tf_op jit(solution)/shard_map/ppermute | solution.py:282
Sparse Core Ops, SparseCore 0:
  25.1 42.7 all-gather.2

commit v4 on v3

v4 whole, which is shorter than its diff:
```python
import functools
import math

import jax
import jax.numpy as jnp
from jax import lax
from jax.experimental import pallas as pl
from jax.experimental.pallas import tpu as pltpu
from jax.sharding import PartitionSpec as P

ITERS = 4
EPS = 0.01
CORES, XS = 2, 4
SHIFT = 24.0 * math.log(2.0)
SCALE = 2.0**48
F32, BF16 = jnp.float32, jnp.bfloat16
VM = pl.BlockSpec(memory_space=pltpu.VMEM)


def params(mib):
    return pltpu.CompilerParams(vmem_limit_bytes=mib * 2**20)


def in_vmem(shape, dtype):
    return pltpu.VMEM(shape, dtype)


def call(body, outs, count, scratch=(), mib=32, name=None):
    return pl.pallas_call(
        body,
        out_shape=outs,
        in_specs=[VM] * count,
        out_specs=jax.tree.map(lambda _: VM, outs, is_leaf=lambda o: hasattr(o, "dtype")),
        scratch_shapes=list(scratch),
        compiler_params=params(mib),
        name=name,
    )


def lanes_to_rows(vec, out_ref):
    for r in range(vec.shape[0]):
        block = jnp.broadcast_to(vec[r : r + 1, :], (128, 128))
        out_ref[r * 128 : (r + 1) * 128, :] = block.T


def rows_to_lanes(ref):
    parts = []
    for r in range(ref.shape[0] // 128):
        parts.append(jnp.sum(ref[r * 128 : (r + 1) * 128, :].T, axis=0, keepdims=True))
    return jnp.concatenate(parts, axis=0)


def flat(vec):
    return jnp.concatenate([vec[t : t + 1, :] for t in range(vec.shape[0])], axis=1)


def lane_sum(val):
    total = val[:, 0:128]
    for t in range(1, val.shape[1] // 128):
        total = total + val[:, t * 128 : (t + 1) * 128]
    return total


def parts_of(refs):
    parts = []
    for ref in refs:
        if len(ref.shape) == 3:
            parts += [ref[k] for k in range(ref.shape[0])]
        else:
            parts.append(ref[...])
    return parts


def merged(refs):
    parts = parts_of(refs)
    top = functools.reduce(jnp.maximum, parts)
    return top + jnp.log(sum(jnp.exp(part - top) for part in parts))


def added(refs):
    return functools.reduce(jnp.add, [part.astype(F32) for part in parts_of(refs)])


def half_at(flip, rows):
    return pl.multiple_of(lax.rem(lax.axis_index("c") + flip, 2) * rows, rows)


def noise_body(parts, out):
    for r in range(out.shape[0] // 128):
        at = slice(r * 128, (r + 1) * 128)
        blocks = [parts[k, :, at].astype(F32).T for k in range(parts.shape[0])]
        out[at, :] = jnp.concatenate(blocks, axis=1).astype(BF16)


def cost_body(noise, data, *refs):
    *before, score, lse, data_sq, rows_sq, part = refs
    rows, depth = noise.shape
    width = 256
    contract = (((1,), (1,)), ((), ()))
    for r in range(rows // 128):
        block = noise[r * 128 : (r + 1) * 128, :].astype(F32)
        total = jnp.sum(lane_sum(block * block), axis=1, keepdims=True)
        rows_sq[r * 128 : (r + 1) * 128, :] = jnp.broadcast_to(total, (128, 128))
    for b in range(data.shape[0] // width):
        at = slice(b * width, (b + 1) * width)
        piece = data[at, :]
        places = slice(b * (width // 128), (b + 1) * (width // 128))
        if before:
            data_sq[places, :] = before[1][places, :]
        else:
            wide = piece.astype(F32)
            part[at, :] = lane_sum(wide * wide)
            data_sq[places, :] = rows_to_lanes(part.at[at, :])
        piece_sq = flat(data_sq[places, :])
        cross = lax.dot_general(noise[...], piece, contract, preferred_element_type=F32)
        sq = jnp.concatenate([rows_sq[...]] * (width // 128), axis=1)
        val = (2.0 * cross - sq - piece_sq) * (1.0 / (depth * EPS))
        score[:, at] = val
        top = jnp.max(val, axis=0, keepdims=True)
        total = jnp.sum(jnp.exp(val - top), axis=0, keepdims=True)
        sums = top + jnp.log(total)
        for t in range(width // 128):
            row = slice(b * (width // 128) + t, b * (width // 128) + t + 1)
            lse[row, :] = sums[:, t * 128 : (t + 1) * 128]
    if before:
        lse[...] = merged([lse, before[0]])


def first_row_body(log_data, n, *refs):
    parts, (own, far, expd, peak, lse, part, tops) = refs[:n], refs[n:]
    rows, cols = expd.shape
    half = own.shape[0]
    pot = jnp.broadcast_to(flat(-log_data - merged(parts)), (8, cols))

    def rows_at(base, r):
        return pl.ds(pl.multiple_of(base + r * 8, 8), 8)

    for flip, score in enumerate((own, far)):
        base = half_at(flip, half)

        def find(r, carry):
            val = score[rows_at(0, r), :] + pot
            part[rows_at(base, r), :] = functools.reduce(
                jnp.maximum, [val[:, t * 128 : (t + 1) * 128] for t in range(cols // 128)]
            )
            return carry

        lax.fori_loop(0, half // 8, find, 0, unroll=8)
    high = jnp.concatenate(
        [
            jnp.max(part[r * 128 : (r + 1) * 128, :].T, axis=0, keepdims=True)
            for r in range(rows // 128)
        ],
        axis=0,
    )
    lanes_to_rows(high - SHIFT, tops)
    for flip, score in enumerate((own, far)):
        base = half_at(flip, half)

        def raise_up(r, carry):
            at = rows_at(base, r)
            top = jnp.concatenate([tops[at, :]] * (cols // 128), axis=1)
            e = jnp.exp((score[rows_at(0, r), :] + pot) - top)
            expd[at, :] = e
            part[at, :] = lane_sum(e)
            return carry

        lax.fori_loop(0, half // 8, raise_up, 0, unroll=8)
    peak[...] = high
    lse[...] = high + (jnp.log(rows_to_lanes(part)) - SHIFT)


def column_sums(expd, factor, factors, out):
    lanes_to_rows(factor, factors)
    rows, cols = expd.shape
    copies = cols // 128

    def body(r, acc):
        at = pl.ds(pl.multiple_of(r * 8, 8), 8)
        f = factors[at, :]
        return acc + expd[at, :] * jnp.concatenate([f] * copies, axis=1)

    acc = lax.fori_loop(0, rows // 8, body, jnp.zeros((8, cols), F32), unroll=8)
    sums = jnp.sum(acc, axis=0, keepdims=True)
    count, width = out.shape
    rows_out = factors.at[0:count, :]
    for t in range(count):
        rows_out[t : t + 1, :] = sums[:, t * width : (t + 1) * width]
    out[...] = rows_out[...].astype(out.dtype)


def first_col_body(count, n, *refs):
    parts, (peak, expd, out, scale, factors) = refs[:n], refs[n:]
    s = jnp.exp(peak[...] - merged(parts) + SHIFT)
    scale[...] = s
    column_sums(expd, s * (1.0 / count), factors, out)


def col_body(count, n, *refs):
    parts, (scale, expd, out, *factor, factors) = refs[:n], refs[n:]
    f = scale[...] * ((SCALE / count) / added(parts))
    for ref in factor:
        ref[...] = f
    column_sums(expd, f, factors, out)


def row_body(count, n, *refs):
    parts, (scale, expd, out, part) = refs[:n], refs[n:]
    v = jnp.broadcast_to(flat((SCALE / count) / added(parts)), (8, expd.shape[1]))
    rows = expd.shape[0]

    def body(r, carry):
        at = pl.ds(pl.multiple_of(r * 8, 8), 8)
        part[at, :] = lane_sum(expd[at, :] * v)
        return carry

    lax.fori_loop(0, rows // 8, body, 0, unroll=8)
    out[...] = (rows_to_lanes(part) * scale[...]).astype(out.dtype)


def split_three(mass, deep):
    high = mass.astype(BF16).astype(F32)
    mid = (mass - high).astype(BF16).astype(F32)
    zero = jnp.zeros((deep - 3, mass.shape[1]), F32)
    return jnp.concatenate([high, mid, mass - high - mid, zero], axis=0)


def add_three(tail):
    return tail[0:1, :] + tail[1:2, :] + tail[2:3, :]


def target_body(count, flip, n, *refs):
    parts, (factor, expd, data, out) = refs[:n], refs[n : n + 4]
    *mass, part, factors = refs[n + 4 :]
    v = jnp.broadcast_to(flat((SCALE / count) / added(parts)), (128, expd.shape[1]))
    half, wide = factors.shape[0], expd.shape[1]
    base = half_at(flip, half)
    first = lax.rem(lax.axis_index("c") + flip, 2) * (half // 128)
    lanes_to_rows(factor[pl.ds(first, half // 128), :], factors)
    cols, deep, _ = out.shape
    depth = data.shape[1] // cols
    for r in range(half // 128):
        at = slice(r * 128, (r + 1) * 128)
        f = jnp.concatenate([factors[at, :]] * (wide // 128), axis=1)
        w = expd[pl.ds(pl.multiple_of(base + r * 128, 128), 128), :] * v * f
        total = jnp.sum(lane_sum(w).T, axis=0, keepdims=True)
        part[r : r + 1, :] = total
        block = jnp.dot(w.astype(BF16), data[...], preferred_element_type=F32).T
        tail = [] if mass else [split_three(total, deep - depth)]
        for k in range(cols):
            rows = [block[k * depth : (k + 1) * depth, :]] + tail
            out[k, :, at] = jnp.concatenate(rows, axis=0).astype(out.dtype)
    for ref in mass:
        ref[...] = part[...]


def pack_body(own, mass, far, out):
    depth, deep = own.shape[1], out.shape[1]
    parts = [far[k].astype(F32) for k in range(out.shape[0])]
    tail = split_three(flat(mass[...]) + add_three(parts[0][depth:deep, :]), deep - depth)
    for k, part in enumerate(parts):
        out[k] = jnp.concatenate([own[k] + part[0:depth, :], tail], axis=0).astype(BF16)


def finish_body(parts, out):
    depth = out.shape[0]
    total = functools.reduce(jnp.add, [parts[k].astype(F32) for k in range(parts.shape[0])])
    out[...] = (total[0:depth, :] / add_three(total[depth:, :])).astype(BF16)


def spread_body(val, out):
    for k in range(out.shape[0]):
        out[k] = val[...]


def everyone(val, axes):
    count = lax.axis_size(axes)
    copies = jnp.broadcast_to(val[None], (count,) + val.shape)
    return lax.all_to_all(copies, axes, 0, 0, tiled=True)


def swapped(val):
    return lax.ppermute(val, "c", [(0, 1), (1, 0)])


def on_device(noise, data, *, vmem=in_vmem):
    zs, xs, cs, cols_all = (lax.axis_size(a) for a in ("z", "x", "c", "col"))
    half, slice_width = noise.shape
    rows = half * cs
    depth = slice_width * cols_all
    wide = data.shape[0] * zs * xs
    count_noise, count_data = float(rows * zs * xs), float(wide * cs * cols_all)
    log_data = math.log(count_data)
    row_axes, col_axes = ("z", "x"), ("col", "c")

    noise_parts = lax.all_gather(noise.T, "col", axis=0)
    copies = call(spread_body, vmem((zs * xs,) + data.shape, BF16), 1, name="spread")(data)
    data_all = lax.all_to_all(copies, row_axes, 0, 0, tiled=True).reshape(wide, depth)
    own = call(noise_body, jax.ShapeDtypeStruct((half, depth), BF16), 1, name="noise")(noise_parts)
    far = swapped(own)

    vec_col = jax.ShapeDtypeStruct((wide // 128, 128), F32)
    sent_col = jax.ShapeDtypeStruct((wide // 128, 128), BF16)
    sent_row = jax.ShapeDtypeStruct((rows // 128, 128), BF16)
    vec_row = jax.ShapeDtypeStruct((rows // 128, 128), F32)
    strip = pltpu.VMEM((rows, 128), F32)

    cost_outs = (vmem((half, wide), F32), vec_col, vec_col)
    cost_scratch = [pltpu.VMEM((half, 128), F32), pltpu.VMEM((wide, 128), F32)]
    score_own, *before = call(cost_body, cost_outs, 2, cost_scratch, name="cost_own")(own, data_all)
    score_far, lse, _ = call(cost_body, cost_outs, 4, cost_scratch, name="cost_far")(far, data_all, *before)
    parts = everyone(lse, row_axes)
    expd, peak, lse = call(
        functools.partial(first_row_body, log_data, 1),
        (vmem((rows, wide), F32), vec_row, vec_row), 3, [strip, strip], name="first_rows",
    )(parts, score_own, score_far)
    parts = everyone(lse, col_axes)
    sums, scale = call(
        functools.partial(first_col_body, count_noise, 1),
        (sent_col, vec_row), 3, [strip], name="first_cols",
    )(parts, peak, expd)
    for sweep in range(1, ITERS - 1):
        parts = everyone(sums, row_axes)
        mass = call(
            functools.partial(row_body, count_data, 1), sent_row, 3, [strip], name="rows"
        )(parts, scale, expd)
        parts = everyone(mass, col_axes)
        last = sweep == ITERS - 2
        sums, *factor = call(
            functools.partial(col_body, count_noise, 1),
            (sent_col, vec_row) if last else (sent_col,), 3, [strip], name="cols",
        )(parts, scale, expd)
    (factor,) = factor
    parts = everyone(sums, row_axes)

    strips = [pltpu.VMEM((half // 128, 128), F32), pltpu.VMEM((half, 128), F32)]
    packed = jax.ShapeDtypeStruct((cols_all, slice_width + 8, half), BF16)
    far = call(
        functools.partial(target_body, count_data, 1, 1), packed, 4, strips, name="targets_far"
    )(parts, factor, expd, data_all)
    far = swapped(far)
    mine, mass = call(
        functools.partial(target_body, count_data, 0, 1),
        (vmem((cols_all, slice_width, half), F32), jax.ShapeDtypeStruct((half // 128, 128), F32)),
        4, strips, name="targets_own",
    )(parts, factor, expd, data_all)
    pieces = call(pack_body, packed, 3, name="pack")(mine, mass, far)
    got = lax.all_to_all(pieces, "col", 0, 0, tiled=True)
    out = call(finish_body, jax.ShapeDtypeStruct((slice_width, half), BF16), 1, name="finish")(got)
    return out.T


def solution(mesh):
    rows, cols = mesh.devices.shape
    parts = (rows // (XS * CORES), XS, CORES, cols)
    split = jax.sharding.Mesh(mesh.devices.reshape(parts), ("z", "x", "c", "col"))
    return jax.shard_map(
        on_device,
        mesh=split,
        in_specs=(P(("z", "x", "c"), "col"), P(("col", "z", "x", "c"), None)),
        out_specs=P(("z", "x", "c"), "col"),
        check_vma=False,
    )
```

time: 211 us -> 176 us (0.83)
  waiting for transfers between devices: 46.1 us -> 0.92 us
  blocking collectives: 119 us -> 137 us
  between operations: 13.5 us -> 0.14 us
  starting transfers between devices: 17.2 us -> 24.7 us
  local copies, waits for them, and re-layouts: 3.14 us -> 0.83 us
    all_gather x1 -> x0, waiting for transfers between devices: 45.1 us -> none  [on_device(): noise_parts = lax.all_gather(noise.T, ('col', 'c'), axis=0)]
    all_gather x0 -> x1, blocking collectives: none -> 22.5 us  [on_device(): noise_parts = lax.all_gather(noise.T, 'col', axis=0)]
    ppermute x1 -> x2, starting transfers between devices: 3.47 us -> 11 us  [swapped(): return lax.ppermute(val, 'c', [(0, 1), (1, 0)])]
    all_to_all x7, blocking collectives: 95.4 us -> 92.4 us  [everyone(): return lax.all_to_all(copies, axes, 0, 0, tiled=True)]
    pallas_call x8 -> x10, Pallas kernels: 8.14 us -> 9.08 us  [the longest x1 2.05 us: on_device(): call(functools.partial(first_row_body, log_data, 1), (vmem((rows, wide),...]
  transfers between devices with their start and end apart: 3 -> 3, of which waited for: 2 -> 2; matrix products, arithmetic and copies ran while one was open for 0% -> 0% of each run, Pallas kernels for 1% -> 2%
where the time goes in v4:
time: 176 us; the launch traced here: 175 us
  blocking collectives  137 us (78%)
  starting transfers between devices  24.7 us (14%)
  Pallas kernels  11.9 us (7%)
    all_to_all x7, blocking collectives, everyone(): return lax.all_to_all(copies, axes, 0, 0, tiled=True)  92.4 us
    all_gather x1, blocking collectives, on_device(): noise_parts = lax.all_gather(noise.T, 'col', axis=0)  22.5 us
    all_to_all x1, blocking collectives, on_device(): got = lax.all_to_all(pieces, 'col', 0, 0, tiled=True)  21.8 us
    all_to_all x1, starting transfers between devices, on_device(): lax.all_to_all(copies, row_axes, 0, 0, tiled=True).reshape(wide, depth)  13.7 us
    ppermute x2, starting transfers between devices, swapped(): return lax.ppermute(val, 'c', [(0, 1), (1, 0)])  11 us
  transfers between devices with their start and end apart: 3, of which 2 were waited for; matrix products, arithmetic and copies ran while one was open for 0% of the time, Pallas kernels for 2%

profile of v4, /device:TPU:1, one launch (start us, length us, event | category | flops | bytes accessed | tf_op | source)
XLA Modules:
  0.0 175.2 jit_solution(8202834887174703726)
XLA Ops:
  0.0 0.0 copy-start
  0.0 0.8 copy-done
  0.8 0.0 copy-start.1
  0.8 1.0 spread.1
  1.8 13.7 %all-to-all-start = ((bf16[32,32,512]{2,1,0:T(8,128)(2,1)}), bf16[32,32,512]{2,1,0:T(8,128)(2,1)S(1)}, u32[]{:S(2)}, u32[]{:S(2)}) async-start(bf16[32,32,512]{2,1,0:T(8,128)(2,1)} %spread.1), calls=%async_computation | async-start | bytes 2097152 | tf_op jit(solution)/shard_map/all_to_all | solution.py:298
  15.5 0.0 copy-done.1
  15.5 22.5 %all-gather = bf16[512,512]{1,0:T(8,128)(2,1)S(1)} all-gather(bf16[64,512]{1,0:T(8,128)(2,1)S(1)} %bitcast.9), channel_id=2, replica_groups=mesh['z'=8,'x'=4,'c'=2,'col'=8] {'col'}, dimensions={0}, use_global_device_ids=true | all-gather | bytes 589824 | tf_op jit(solution)/shard_map/all_gather | solution.py:296
  38.0 0.5 noise.1
  38.6 7.4 %collective-permute-start = (bf16[512,512]{1,0:T(8,128)(2,1)S(1)}, bf16[512,512]{1,0:T(8,128)(2,1)S(1)}, u32[]{:S(2)}, u32[]{:S(2)}) collective-permute-start(bf16[512,512]{1,0:T(8,128)(2,1)S(1)} %noise.1), channel_id=1, source_target_pairs={{0,8},{8,0},{1,9},{9,1},{2,10},{10,2},{3,11},{11,3},{4,12},{12,4},... | collective-permute-start | bytes 1572872 | tf_op jit(solution)/shard_map/ppermute | solution.py:283
  46.0 0.0 all-to-all-done
  46.0 1.2 cost_own.1
  47.2 0.3 collective-permute-done.noise
  47.5 1.2 cost_far.1
  48.8 18.6 %all_to_all.45.refs_0_ = f32[32,8,128]{2,1,0:T(8,128)S(1)} all-to-all(f32[32,8,128]{2,1,0:T(8,128)S(1)} %broadcast_in_dim.14), channel_id=1, replica_groups=mesh['z'=8,'x'=4,'c'=2,'col'=8] {'z','x'}, dimensions={0} | all-to-all | bytes 262144 | tf_op jit(solution)/shard_map/all_to_all | solution.py:279
  67.4 2.1 %first_rows.1 = (f32[1024,1024]{1,0:T(8,128)S(1)}, f32[8,128]{1,0:T(8,128)S(1)}, f32[8,128]{1,0:T(8,128)S(1)}) custom-call(f32[32,8,128]{2,1,0:T(8,128)S(1)} %all_to_all.45.refs_0_, f32[512,1024]{1,0:T(8,128)S(1)} %get-tuple-element.22.refs_1_, f32[512,1024]{1,0:T(8,128)S(1)} %get-tuple-element.23.refs_2_), custom_call_target="tpu_custom_call" | custom-call | tf_op jit(solution)/shard_map/first_rows/pallas_call | solution.py:313
  69.5 15.3 %all_to_all.46.refs_0_ = f32[16,8,128]{2,1,0:T(8,128)S(1)} all-to-all(f32[16,8,128]{2,1,0:T(8,128)S(1)} %broadcast_in_dim.15), channel_id=1, replica_groups=mesh['z'=8,'x'=4,'c'=2,'col'=8] {'col','c'}, dimensions={0} | all-to-all | bytes 131072 | tf_op jit(solution)/shard_map/all_to_all | solution.py:279
  84.8 0.6 first_cols.1
  85.4 11.9 %all_to_all.47.refs_0_ = bf16[32,8,128]{2,1,0:T(8,128)(2,1)S(1)} all-to-all(bf16[32,8,128]{2,1,0:T(8,128)(2,1)S(1)} %broadcast_in_dim.16), channel_id=1, replica_groups=mesh['z'=8,'x'=4,'c'=2,'col'=8] {'z','x'}, dimensions={0} | all-to-all | bytes 131072 | tf_op jit(solution)/shard_map/all_to_all | solution.py:279
  97.3 0.6 rows.2
  97.9 11.4 %all_to_all.48.refs_0_ = bf16[16,8,128]{2,1,0:T(8,128)(2,1)S(1)} all-to-all(bf16[16,8,128]{2,1,0:T(8,128)(2,1)S(1)} %broadcast_in_dim.17), channel_id=1, replica_groups=mesh['z'=8,'x'=4,'c'=2,'col'=8] {'col','c'}, dimensions={0} | all-to-all | bytes 65536 | tf_op jit(solution)/shard_map/all_to_all | solution.py:279
  109.3 0.6 cols.2
  110.0 11.8 %all_to_all.49.refs_0_ = bf16[32,8,128]{2,1,0:T(8,128)(2,1)S(1)} all-to-all(bf16[32,8,128]{2,1,0:T(8,128)(2,1)S(1)} %broadcast_in_dim.18), channel_id=1, replica_groups=mesh['z'=8,'x'=4,'c'=2,'col'=8] {'z','x'}, dimensions={0} | all-to-all | bytes 131072 | tf_op jit(solution)/shard_map/all_to_all | solution.py:279
  121.8 0.6 rows.3
  122.4 11.5 %all_to_all.50.refs_0_ = bf16[16,8,128]{2,1,0:T(8,128)(2,1)S(1)} all-to-all(bf16[16,8,128]{2,1,0:T(8,128)(2,1)S(1)} %broadcast_in_dim.19), channel_id=1, replica_groups=mesh['z'=8,'x'=4,'c'=2,'col'=8] {'col','c'}, dimensions={0} | all-to-all | bytes 65536 | tf_op jit(solution)/shard_map/all_to_all | solution.py:279
  133.9 0.6 cols.3
  134.6 11.8 %all_to_all.51.refs_0_ = bf16[32,8,128]{2,1,0:T(8,128)(2,1)S(1)} all-to-all(bf16[32,8,128]{2,1,0:T(8,128)(2,1)S(1)} %broadcast_in_dim.20), channel_id=1, replica_groups=mesh['z'=8,'x'=4,'c'=2,'col'=8] {'z','x'}, dimensions={0} | all-to-all | bytes 131072 | tf_op jit(solution)/shard_map/all_to_all | solution.py:279
  146.4 1.0 targets_far.1
  147.4 3.5 %collective-permute-start.1 = (bf16[8,72,512]{2,1,0:T(8,128)(2,1)S(1)}, bf16[8,72,512]{2,1,0:T(8,128)(2,1)S(1)}, u32[]{:S(2)}, u32[]{:S(2)}) collective-permute-start(bf16[8,72,512]{2,1,0:T(8,128)(2,1)S(1)} %targets_far.1), channel_id=1, source_target_pairs={{0,8},{8,0},{1,9},{9,1},{2,10},{10,2},{3,11},{11,3},{4,12},{12,4},... | collective-permute-start | bytes 1769480 | tf_op jit(solution)/shard_map/ppermute | solution.py:283
  150.9 1.0 targets_own.1
  152.0 0.6 collective-permute-done.1.far
  152.6 0.1 pack.1
  152.7 21.8 %all_to_all.52.parts = bf16[8,72,512]{2,1,0:T(8,128)(2,1)S(1)} all-to-all(bf16[8,72,512]{2,1,0:T(8,128)(2,1)S(1)} %pack.1), channel_id=1, replica_groups=mesh['z'=8,'x'=4,'c'=2,'col'=8] {'col'}, dimensions={0} | all-to-all | bytes 1179648 | tf_op jit(solution)/shard_map/all_to_all | solution.py:348
  174.4 0.7 finish.1
  (7 shorter events, 0.1 us)
Async XLA Ops:
  0.0 0.8 copy-start
  0.8 14.8 %copy-start.1 = (bf16[512,64]{0,1:T(8,128)(2,1)S(1)}, bf16[512,64]{0,1:T(8,128)(2,1)}, u32[]{:S(2)}) copy-start(bf16[512,64]{0,1:T(8,128)(2,1)} %param.2) | copy-start | bytes 196612
  1.8 44.2 %all-to-all-start = ((bf16[32,32,512]{2,1,0:T(8,128)(2,1)}), bf16[32,32,512]{2,1,0:T(8,128)(2,1)S(1)}, u32[]{:S(2)}, u32[]{:S(2)}) async-start(bf16[32,32,512]{2,1,0:T(8,128)(2,1)} %spread.1), calls=%async_computation | async-start | bytes 2097152 | tf_op jit(solution)/shard_map/all_to_all | solution.py:298
  38.6 9.0 %collective-permute-start = (bf16[512,512]{1,0:T(8,128)(2,1)S(1)}, bf16[512,512]{1,0:T(8,128)(2,1)S(1)}, u32[]{:S(2)}, u32[]{:S(2)}) collective-permute-start(bf16[512,512]{1,0:T(8,128)(2,1)S(1)} %noise.1), channel_id=1, source_target_pairs={{0,8},{8,0},{1,9},{9,1},{2,10},{10,2},{3,11},{11,3},{4,12},{12,4},... | collective-permute-start | bytes 1572872 | tf_op jit(solution)/shard_map/ppermute | solution.py:283
  147.4 5.2 %collective-permute-start.1 = (bf16[8,72,512]{2,1,0:T(8,128)(2,1)S(1)}, bf16[8,72,512]{2,1,0:T(8,128)(2,1)S(1)}, u32[]{:S(2)}, u32[]{:S(2)}) collective-permute-start(bf16[8,72,512]{2,1,0:T(8,128)(2,1)S(1)} %targets_far.1), channel_id=1, source_target_pairs={{0,8},{8,0},{1,9},{9,1},{2,10},{10,2},{3,11},{11,3},{4,12},{12,4},... | collective-permute-start | bytes 1769480 | tf_op jit(solution)/shard_map/ppermute | solution.py:283

commit v5 on v4

--- a/solution.py
+++ b/solution.py
@@ -11,7 +11,7 @@
 ITERS = 4
 EPS = 0.01
 CORES, XS = 2, 4
-SHIFT = 24.0 * math.log(2.0)
+SHIFT = 24.0
 SCALE = 2.0**48
 F32, BF16 = jnp.float32, jnp.bfloat16
 VM = pl.BlockSpec(memory_space=pltpu.VMEM)
@@ -74,7 +74,7 @@
 def merged(refs):
     parts = parts_of(refs)
     top = functools.reduce(jnp.maximum, parts)
-    return top + jnp.log(sum(jnp.exp(part - top) for part in parts))
+    return top + jnp.log2(sum(jnp.exp2(part - top) for part in parts))
 
 
 def added(refs):
@@ -96,11 +96,12 @@
     *before, score, lse, data_sq, rows_sq, part = refs
     rows, depth = noise.shape
     width = 256
+    factor = math.log2(math.e) / (depth * EPS)
     contract = (((1,), (1,)), ((), ()))
     for r in range(rows // 128):
         block = noise[r * 128 : (r + 1) * 128, :].astype(F32)
         total = jnp.sum(lane_sum(block * block), axis=1, keepdims=True)
-        rows_sq[r * 128 : (r + 1) * 128, :] = jnp.broadcast_to(total, (128, 128))
+        rows_sq[r * 128 : (r + 1) * 128, :] = jnp.broadcast_to(total * factor, (128, 128))
     for b in range(data.shape[0] // width):
         at = slice(b * width, (b + 1) * width)
         piece = data[at, :]
@@ -110,15 +111,15 @@
         else:
             wide = piece.astype(F32)
             part[at, :] = lane_sum(wide * wide)
-            data_sq[places, :] = rows_to_lanes(part.at[at, :])
+            data_sq[places, :] = rows_to_lanes(part.at[at, :]) * factor
         piece_sq = flat(data_sq[places, :])
         cross = lax.dot_general(noise[...], piece, contract, preferred_element_type=F32)
         sq = jnp.concatenate([rows_sq[...]] * (width // 128), axis=1)
-        val = (2.0 * cross - sq - piece_sq) * (1.0 / (depth * EPS))
+        val = cross * (2.0 * factor) - sq - piece_sq
         score[:, at] = val
         top = jnp.max(val, axis=0, keepdims=True)
-        total = jnp.sum(jnp.exp(val - top), axis=0, keepdims=True)
-        sums = top + jnp.log(total)
+        total = jnp.sum(jnp.exp2(val - top), axis=0, keepdims=True)
+        sums = top + jnp.log2(total)
         for t in range(width // 128):
             row = slice(b * (width // 128) + t, b * (width // 128) + t + 1)
             lse[row, :] = sums[:, t * 128 : (t + 1) * 128]
@@ -160,14 +161,14 @@
         def raise_up(r, carry):
             at = rows_at(base, r)
             top = jnp.concatenate([tops[at, :]] * (cols // 128), axis=1)
-            e = jnp.exp((score[rows_at(0, r), :] + pot) - top)
+            e = jnp.exp2((score[rows_at(0, r), :] + pot) - top)
             expd[at, :] = e
             part[at, :] = lane_sum(e)
             return carry
 
         lax.fori_loop(0, half // 8, raise_up, 0, unroll=8)
     peak[...] = high
-    lse[...] = high + (jnp.log(rows_to_lanes(part)) - SHIFT)
+    lse[...] = high + (jnp.log2(rows_to_lanes(part)) - SHIFT)
 
 
 def column_sums(expd, factor, factors, out):
@@ -191,7 +192,7 @@
 
 def first_col_body(count, n, *refs):
     parts, (peak, expd, out, scale, factors) = refs[:n], refs[n:]
-    s = jnp.exp(peak[...] - merged(parts) + SHIFT)
+    s = jnp.exp2(peak[...] - merged(parts) + SHIFT)
     scale[...] = s
     column_sums(expd, s * (1.0 / count), factors, out)
 
@@ -268,9 +269,32 @@
     out[...] = (total[0:depth, :] / add_three(total[depth:, :])).astype(BF16)
 
 
-def spread_body(val, out):
-    for k in range(out.shape[0]):
-        out[k] = val[...]
+def spread_body(val, out, held, sem_in, sems):
+    come = pltpu.make_async_copy(val, held, sem_in)
+    come.start()
+    come.wait()
+    copies = [pltpu.make_async_copy(held, out.at[k], sems.at[k]) for k in range(out.shape[0])]
+    for copy in copies:
+        copy.start()
+    for copy in copies:
+        copy.wait()
+
+
+def spread(val, count):
+    whole = pl.BlockSpec(memory_space=pl.ANY)
+    return pl.pallas_call(
+        spread_body,
+        out_shape=jax.ShapeDtypeStruct((count,) + val.shape, val.dtype),
+        in_specs=[whole],
+        out_specs=whole,
+        scratch_shapes=[
+            pltpu.VMEM(val.shape, val.dtype),
+            pltpu.SemaphoreType.DMA,
+            pltpu.SemaphoreType.DMA((count,)),
+        ],
+        compiler_params=params(32),
+        name="spread",
+    )(val)
 
 
 def everyone(val, axes):
@@ -290,11 +314,11 @@
     depth = slice_width * cols_all
     wide = data.shape[0] * zs * xs
     count_noise, count_data = float(rows * zs * xs), float(wide * cs * cols_all)
-    log_data = math.log(count_data)
+    log_data = math.log2(count_data)
     row_axes, col_axes = ("z", "x"), ("col", "c")
 
     noise_parts = lax.all_gather(noise.T, "col", axis=0)
-    copies = call(spread_body, vmem((zs * xs,) + data.shape, BF16), 1, name="spread")(data)
+    copies = spread(data, zs * xs)
     data_all = lax.all_to_all(copies, row_axes, 0, 0, tiled=True).reshape(wide, depth)
     own = call(noise_body, jax.ShapeDtypeStruct((half, depth), BF16), 1, name="noise")(noise_parts)
     far = swapped(own)

time: 176 us -> 176 us (level)
  transfers between devices with their start and end apart: 3 -> 3, of which waited for: 2 -> 2; matrix products, arithmetic and copies ran while one was open for 0% -> 0% of each run, Pallas kernels for 2% -> 1%
where the time goes in v5:
time: 176 us; the launch traced here: 175 us
  blocking collectives  137 us (78%)
  starting transfers between devices  24.7 us (14%)
  Pallas kernels  12.1 us (7%)
    all_to_all x7, blocking collectives, everyone(): return lax.all_to_all(copies, axes, 0, 0, tiled=True)  92.4 us
    all_gather x1, blocking collectives, on_device(): noise_parts = lax.all_gather(noise.T, 'col', axis=0)  22.5 us
    all_to_all x1, blocking collectives, on_device(): got = lax.all_to_all(pieces, 'col', 0, 0, tiled=True)  21.8 us
    all_to_all x1, starting transfers between devices, on_device(): lax.all_to_all(copies, row_axes, 0, 0, tiled=True).reshape(wide, depth)  13.7 us
    ppermute x2, starting transfers between devices, swapped(): return lax.ppermute(val, 'c', [(0, 1), (1, 0)])  11 us
  transfers between devices with their start and end apart: 3, of which 2 were waited for; matrix products, arithmetic and copies ran while one was open for 0% of the time, Pallas kernels for 1%

profile of v5, /device:TPU:1, one launch (start us, length us, event | category | flops | bytes accessed | tf_op | source)
XLA Modules:
  0.0 175.4 jit_solution(8629150252683691800)
XLA Ops:
  0.0 0.0 copy-start
  0.0 0.8 copy-done
  0.8 0.0 copy-start.1
  0.8 1.3 spread.1
  2.1 13.7 %all-to-all-start = ((bf16[32,32,512]{2,1,0:T(8,128)(2,1)}), bf16[32,32,512]{2,1,0:T(8,128)(2,1)S(1)}, u32[]{:S(2)}, u32[]{:S(2)}) async-start(bf16[32,32,512]{2,1,0:T(8,128)(2,1)} %spread.1), calls=%async_computation | async-start | bytes 2097152 | tf_op jit(solution)/shard_map/all_to_all | solution.py:322
  15.8 0.0 copy-done.1
  15.8 22.5 %all-gather = bf16[512,512]{1,0:T(8,128)(2,1)S(1)} all-gather(bf16[64,512]{1,0:T(8,128)(2,1)S(1)} %bitcast.9), channel_id=2, replica_groups=mesh['z'=8,'x'=4,'c'=2,'col'=8] {'col'}, dimensions={0}, use_global_device_ids=true | all-gather | bytes 589824 | tf_op jit(solution)/shard_map/all_gather | solution.py:320
  38.3 0.5 noise.1
  38.8 7.4 %collective-permute-start = (bf16[512,512]{1,0:T(8,128)(2,1)S(1)}, bf16[512,512]{1,0:T(8,128)(2,1)S(1)}, u32[]{:S(2)}, u32[]{:S(2)}) collective-permute-start(bf16[512,512]{1,0:T(8,128)(2,1)S(1)} %noise.1), channel_id=1, source_target_pairs={{0,8},{8,0},{1,9},{9,1},{2,10},{10,2},{3,11},{11,3},{4,12},{12,4},... | collective-permute-start | bytes 1572872 | tf_op jit(solution)/shard_map/ppermute | solution.py:307
  46.3 0.0 all-to-all-done
  46.3 1.1 cost_own.1
  47.4 0.4 collective-permute-done.noise
  47.8 1.2 cost_far.1
  49.0 18.6 %all_to_all.45.refs_0_ = f32[32,8,128]{2,1,0:T(8,128)S(1)} all-to-all(f32[32,8,128]{2,1,0:T(8,128)S(1)} %broadcast_in_dim.14), channel_id=1, replica_groups=mesh['z'=8,'x'=4,'c'=2,'col'=8] {'z','x'}, dimensions={0} | all-to-all | bytes 262144 | tf_op jit(solution)/shard_map/all_to_all | solution.py:303
  67.6 2.0 %first_rows.1 = (f32[1024,1024]{1,0:T(8,128)S(1)}, f32[8,128]{1,0:T(8,128)S(1)}, f32[8,128]{1,0:T(8,128)S(1)}) custom-call(f32[32,8,128]{2,1,0:T(8,128)S(1)} %all_to_all.45.refs_0_, f32[512,1024]{1,0:T(8,128)S(1)} %get-tuple-element.22.refs_1_, f32[512,1024]{1,0:T(8,128)S(1)} %get-tuple-element.23.refs_2_), custom_call_target="tpu_custom_call" | custom-call | tf_op jit(solution)/shard_map/first_rows/pallas_call | solution.py:337
  69.7 15.3 %all_to_all.46.refs_0_ = f32[16,8,128]{2,1,0:T(8,128)S(1)} all-to-all(f32[16,8,128]{2,1,0:T(8,128)S(1)} %broadcast_in_dim.15), channel_id=1, replica_groups=mesh['z'=8,'x'=4,'c'=2,'col'=8] {'col','c'}, dimensions={0} | all-to-all | bytes 131072 | tf_op jit(solution)/shard_map/all_to_all | solution.py:303
  85.0 0.6 first_cols.1
  85.6 11.9 %all_to_all.47.refs_0_ = bf16[32,8,128]{2,1,0:T(8,128)(2,1)S(1)} all-to-all(bf16[32,8,128]{2,1,0:T(8,128)(2,1)S(1)} %broadcast_in_dim.16), channel_id=1, replica_groups=mesh['z'=8,'x'=4,'c'=2,'col'=8] {'z','x'}, dimensions={0} | all-to-all | bytes 131072 | tf_op jit(solution)/shard_map/all_to_all | solution.py:303
  97.5 0.6 rows.2
  98.1 11.4 %all_to_all.48.refs_0_ = bf16[16,8,128]{2,1,0:T(8,128)(2,1)S(1)} all-to-all(bf16[16,8,128]{2,1,0:T(8,128)(2,1)S(1)} %broadcast_in_dim.17), channel_id=1, replica_groups=mesh['z'=8,'x'=4,'c'=2,'col'=8] {'col','c'}, dimensions={0} | all-to-all | bytes 65536 | tf_op jit(solution)/shard_map/all_to_all | solution.py:303
  109.6 0.6 cols.2
  110.2 11.8 %all_to_all.49.refs_0_ = bf16[32,8,128]{2,1,0:T(8,128)(2,1)S(1)} all-to-all(bf16[32,8,128]{2,1,0:T(8,128)(2,1)S(1)} %broadcast_in_dim.18), channel_id=1, replica_groups=mesh['z'=8,'x'=4,'c'=2,'col'=8] {'z','x'}, dimensions={0} | all-to-all | bytes 131072 | tf_op jit(solution)/shard_map/all_to_all | solution.py:303
  122.0 0.6 rows.3
  122.7 11.5 %all_to_all.50.refs_0_ = bf16[16,8,128]{2,1,0:T(8,128)(2,1)S(1)} all-to-all(bf16[16,8,128]{2,1,0:T(8,128)(2,1)S(1)} %broadcast_in_dim.19), channel_id=1, replica_groups=mesh['z'=8,'x'=4,'c'=2,'col'=8] {'col','c'}, dimensions={0} | all-to-all | bytes 65536 | tf_op jit(solution)/shard_map/all_to_all | solution.py:303
  134.2 0.6 cols.3
  134.8 11.8 %all_to_all.51.refs_0_ = bf16[32,8,128]{2,1,0:T(8,128)(2,1)S(1)} all-to-all(bf16[32,8,128]{2,1,0:T(8,128)(2,1)S(1)} %broadcast_in_dim.20), channel_id=1, replica_groups=mesh['z'=8,'x'=4,'c'=2,'col'=8] {'z','x'}, dimensions={0} | all-to-all | bytes 131072 | tf_op jit(solution)/shard_map/all_to_all | solution.py:303
  146.6 1.0 targets_far.1
  147.6 3.5 %collective-permute-start.1 = (bf16[8,72,512]{2,1,0:T(8,128)(2,1)S(1)}, bf16[8,72,512]{2,1,0:T(8,128)(2,1)S(1)}, u32[]{:S(2)}, u32[]{:S(2)}) collective-permute-start(bf16[8,72,512]{2,1,0:T(8,128)(2,1)S(1)} %targets_far.1), channel_id=1, source_target_pairs={{0,8},{8,0},{1,9},{9,1},{2,10},{10,2},{3,11},{11,3},{4,12},{12,4},... | collective-permute-start | bytes 1769480 | tf_op jit(solution)/shard_map/ppermute | solution.py:307
  151.2 1.0 targets_own.1
  152.2 0.6 collective-permute-done.1.far
  152.8 0.1 pack.1
  152.9 21.8 %all_to_all.52.parts = bf16[8,72,512]{2,1,0:T(8,128)(2,1)S(1)} all-to-all(bf16[8,72,512]{2,1,0:T(8,128)(2,1)S(1)} %pack.1), channel_id=1, replica_groups=mesh['z'=8,'x'=4,'c'=2,'col'=8] {'col'}, dimensions={0} | all-to-all | bytes 1179648 | tf_op jit(solution)/shard_map/all_to_all | solution.py:372
  174.7 0.7 finish.1
  (7 shorter events, 0.1 us)
Async XLA Ops:
  0.0 0.8 copy-start
  0.8 15.0 %copy-start.1 = (bf16[512,64]{0,1:T(8,128)(2,1)S(1)}, bf16[512,64]{0,1:T(8,128)(2,1)}, u32[]{:S(2)}) copy-start(bf16[512,64]{0,1:T(8,128)(2,1)} %param.2) | copy-start | bytes 196612
  2.1 44.2 %all-to-all-start = ((bf16[32,32,512]{2,1,0:T(8,128)(2,1)}), bf16[32,32,512]{2,1,0:T(8,128)(2,1)S(1)}, u32[]{:S(2)}, u32[]{:S(2)}) async-start(bf16[32,32,512]{2,1,0:T(8,128)(2,1)} %spread.1), calls=%async_computation | async-start | bytes 2097152 | tf_op jit(solution)/shard_map/all_to_all | solution.py:322
  38.8 9.0 %collective-permute-start = (bf16[512,512]{1,0:T(8,128)(2,1)S(1)}, bf16[512,512]{1,0:T(8,128)(2,1)S(1)}, u32[]{:S(2)}, u32[]{:S(2)}) collective-permute-start(bf16[512,512]{1,0:T(8,128)(2,1)S(1)} %noise.1), channel_id=1, source_target_pairs={{0,8},{8,0},{1,9},{9,1},{2,10},{10,2},{3,11},{11,3},{4,12},{12,4},... | collective-permute-start | bytes 1572872 | tf_op jit(solution)/shard_map/ppermute | solution.py:307
  147.6 5.2 %collective-permute-start.1 = (bf16[8,72,512]{2,1,0:T(8,128)(2,1)S(1)}, bf16[8,72,512]{2,1,0:T(8,128)(2,1)S(1)}, u32[]{:S(2)}, u32[]{:S(2)}) collective-permute-start(bf16[8,72,512]{2,1,0:T(8,128)(2,1)S(1)} %targets_far.1), channel_id=1, source_target_pairs={{0,8},{8,0},{1,9},{9,1},{2,10},{10,2},{3,11},{11,3},{4,12},{12,4},... | collective-permute-start | bytes 1769480 | tf_op jit(solution)/shard_map/ppermute | solution.py:307

commit v6 on v5

--- a/solution.py
+++ b/solution.py
@@ -11,6 +11,7 @@
 ITERS = 4
 EPS = 0.01
 CORES, XS = 2, 4
+COL = ("yh", "yl")
 SHIFT = 24.0
 SCALE = 2.0**48
 F32, BF16 = jnp.float32, jnp.bfloat16
@@ -269,11 +270,14 @@
     out[...] = (total[0:depth, :] / add_three(total[depth:, :])).astype(BF16)
 
 
-def spread_body(val, out, held, sem_in, sems):
-    come = pltpu.make_async_copy(val, held, sem_in)
-    come.start()
-    come.wait()
-    copies = [pltpu.make_async_copy(held, out.at[k], sems.at[k]) for k in range(out.shape[0])]
+def pair_body(here, there, out):
+    place = lax.axis_index("yl")
+    out[place] = here[...]
+    out[1 - place] = there[...]
+
+
+def spread_body(val, out, sems):
+    copies = [pltpu.make_async_copy(val, out.at[k], sems.at[k]) for k in range(out.shape[0])]
     for copy in copies:
         copy.start()
     for copy in copies:
@@ -281,17 +285,12 @@
 
 
 def spread(val, count):
-    whole = pl.BlockSpec(memory_space=pl.ANY)
     return pl.pallas_call(
         spread_body,
         out_shape=jax.ShapeDtypeStruct((count,) + val.shape, val.dtype),
-        in_specs=[whole],
-        out_specs=whole,
-        scratch_shapes=[
-            pltpu.VMEM(val.shape, val.dtype),
-            pltpu.SemaphoreType.DMA,
-            pltpu.SemaphoreType.DMA((count,)),
-        ],
+        in_specs=[VM],
+        out_specs=pl.BlockSpec(memory_space=pl.ANY),
+        scratch_shapes=[pltpu.SemaphoreType.DMA((count,))],
         compiler_params=params(32),
         name="spread",
     )(val)
@@ -303,21 +302,23 @@
     return lax.all_to_all(copies, axes, 0, 0, tiled=True)
 
 
-def swapped(val):
-    return lax.ppermute(val, "c", [(0, 1), (1, 0)])
+def swapped(val, axis="c"):
+    return lax.ppermute(val, axis, [(0, 1), (1, 0)])
 
 
 def on_device(noise, data, *, vmem=in_vmem):
-    zs, xs, cs, cols_all = (lax.axis_size(a) for a in ("z", "x", "c", "col"))
+    zs, xs, cs, cols_all = (lax.axis_size(a) for a in ("z", "x", "c", COL))
     half, slice_width = noise.shape
     rows = half * cs
     depth = slice_width * cols_all
     wide = data.shape[0] * zs * xs
     count_noise, count_data = float(rows * zs * xs), float(wide * cs * cols_all)
     log_data = math.log2(count_data)
-    row_axes, col_axes = ("z", "x"), ("col", "c")
-
-    noise_parts = lax.all_gather(noise.T, "col", axis=0)
+    row_axes, col_axes = ("z", "x"), COL + ("c",)
+
+    here = noise.T
+    pair = call(pair_body, jax.ShapeDtypeStruct((2,) + here.shape, BF16), 2, name="pair")(here, swapped(here, "yl"))
+    noise_parts = lax.all_gather(pair, "yh", axis=0).reshape(cols_all, slice_width, half)
     copies = spread(data, zs * xs)
     data_all = lax.all_to_all(copies, row_axes, 0, 0, tiled=True).reshape(wide, depth)
     own = call(noise_body, jax.ShapeDtypeStruct((half, depth), BF16), 1, name="noise")(noise_parts)
@@ -369,19 +370,20 @@
         4, strips, name="targets_own",
     )(parts, factor, expd, data_all)
     pieces = call(pack_body, packed, 3, name="pack")(mine, mass, far)
-    got = lax.all_to_all(pieces, "col", 0, 0, tiled=True)
+    got = lax.all_to_all(pieces, COL, 0, 0, tiled=True)
     out = call(finish_body, jax.ShapeDtypeStruct((slice_width, half), BF16), 1, name="finish")(got)
     return out.T
 
 
 def solution(mesh):
     rows, cols = mesh.devices.shape
-    parts = (rows // (XS * CORES), XS, CORES, cols)
-    split = jax.sharding.Mesh(mesh.devices.reshape(parts), ("z", "x", "c", "col"))
+    parts = (rows // (XS * CORES), XS, CORES, cols // 2, 2)
+    row_split = ("z", "x", "c")
+    split = jax.sharding.Mesh(mesh.devices.reshape(parts), row_split + COL)
     return jax.shard_map(
         on_device,
         mesh=split,
-        in_specs=(P(("z", "x", "c"), "col"), P(("col", "z", "x", "c"), None)),
-        out_specs=P(("z", "x", "c"), "col"),
+        in_specs=(P(row_split, COL), P(COL + row_split, None)),
+        out_specs=P(row_split, COL),
         check_vma=False,
     )

time: 176 us -> 173 us (0.983)
  blocking collectives: 137 us -> 130 us
  waiting for transfers between devices: 0.99 us -> 3.09 us
  starting transfers between devices: 24.7 us -> 26.6 us
    all_gather x1, blocking collectives: 22.5 us -> 16.9 us  [on_device(): lax.all_gather(pair, 'yh', axis=0).reshape(cols_all, slice_width, half)]
    ppermute x2 -> x3, waiting for transfers between devices: 0.99 us -> 3.09 us  [swapped(): return lax.ppermute(val, axis, [(0, 1), (1, 0)])]
    ppermute x2 -> x3, starting transfers between devices: 11 us -> 12.8 us  [swapped(): return lax.ppermute(val, axis, [(0, 1), (1, 0)])]
  transfers between devices with their start and end apart: 3 -> 4, of which waited for: 2 -> 3; matrix products, arithmetic and copies ran while one was open for 0% -> 0% of each run, Pallas kernels for 1% -> 2%
where the time goes in v6:
time: 173 us; the launch traced here: 172 us
  blocking collectives  130 us (75%)
  starting transfers between devices  26.6 us (15%)
  Pallas kernels  12 us (7%)
  waiting for transfers between devices  3.09 us (2%)
    all_to_all x7, blocking collectives, everyone(): return lax.all_to_all(copies, axes, 0, 0, tiled=True)  91.1 us
    all_to_all x1, blocking collectives, on_device(): got = lax.all_to_all(pieces, COL, 0, 0, tiled=True)  21.8 us
    all_gather x1, blocking collectives, on_device(): lax.all_gather(pair, 'yh', axis=0).reshape(cols_all, slice_width, half)  16.9 us
    all_to_all x1, starting transfers between devices, on_device(): lax.all_to_all(copies, row_axes, 0, 0, tiled=True).reshape(wide, depth)  13.7 us
    ppermute x3, starting transfers between devices, swapped(): return lax.ppermute(val, axis, [(0, 1), (1, 0)])  12.8 us
  transfers between devices with their start and end apart: 4, of which 3 were waited for; matrix products, arithmetic and copies ran while one was open for 0% of the time, Pallas kernels for 2%

profile of v6, /device:TPU:1, one launch (start us, length us, event | category | flops | bytes accessed | tf_op | source)
XLA Modules:
  0.0 172.4 jit_solution(2341036233492659781)
XLA Ops:
  0.0 0.0 copy-start.1
  0.0 0.8 copy-done.1
  0.8 0.0 copy-start
  0.8 1.3 spread.1
  2.0 13.7 %all-to-all-start = ((bf16[32,32,512]{2,1,0:T(8,128)(2,1)}), bf16[32,32,512]{2,1,0:T(8,128)(2,1)S(1)}, u32[]{:S(2)}, u32[]{:S(2)}) async-start(bf16[32,32,512]{2,1,0:T(8,128)(2,1)} %spread.1), calls=%async_computation | async-start | bytes 2097152 | tf_op jit(solution)/shard_map/all_to_all | solution.py:323
  15.8 0.0 copy-done
  15.8 3.2 %collective-permute-start = (bf16[64,512]{1,0:T(8,128)(2,1)S(1)}, bf16[64,512]{1,0:T(8,128)(2,1)S(1)}, u32[]{:S(2)}, u32[]{:S(2)}) collective-permute-start(bf16[64,512]{1,0:T(8,128)(2,1)S(1)} %bitcast.7), channel_id=1, source_target_pairs={{0,1},{1,0},{2,3},{3,2},{4,5},{5,4},{6,7},{7,6},{8,9},{9,8},{10,11... | collective-permute-start | bytes 196616 | tf_op jit(solution)/shard_map/ppermute | solution.py:306
  19.0 2.1 %collective-permute-done.there = bf16[64,512]{1,0:T(8,128)(2,1)S(1)} collective-permute-done((bf16[64,512]{1,0:T(8,128)(2,1)S(1)}, bf16[64,512]{1,0:T(8,128)(2,1)S(1)}, u32[]{:S(2)}, u32[]{:S(2)}) %collective-permute-start) | collective-permute-done | bytes 65568 | tf_op jit(solution)/shard_map/ppermute | solution.py:306
  21.1 16.9 %all-gather.parts = bf16[8,64,512]{2,1,0:T(8,128)(2,1)S(1)} all-gather(bf16[2,64,512]{2,1,0:T(8,128)(2,1)S(1)} %pair.1), channel_id=2, replica_groups=mesh['z'=8,'x'=4,'c'=2,'yh'=4,'yl'=2] {'yh'}, dimensions={0}, use_global_device_ids=true | all-gather | bytes 655360 | tf_op jit(solution)/shard_map/all_gather | solution.py:321
  38.0 0.5 noise.1
  38.5 6.1 %collective-permute-start.1 = (bf16[512,512]{1,0:T(8,128)(2,1)S(1)}, bf16[512,512]{1,0:T(8,128)(2,1)S(1)}, u32[]{:S(2)}, u32[]{:S(2)}) collective-permute-start(bf16[512,512]{1,0:T(8,128)(2,1)S(1)} %noise.1), channel_id=1, source_target_pairs={{0,8},{8,0},{1,9},{9,1},{2,10},{10,2},{3,11},{11,3},{4,12},{12,4},... | collective-permute-start | bytes 1572872 | tf_op jit(solution)/shard_map/ppermute | solution.py:306
  44.6 0.0 all-to-all-done
  44.6 1.1 cost_own.1
  45.7 0.4 collective-permute-done.1.noise
  46.1 1.2 cost_far.1
  47.3 18.7 %all_to_all.45.refs_0_ = f32[32,8,128]{2,1,0:T(8,128)S(1)} all-to-all(f32[32,8,128]{2,1,0:T(8,128)S(1)} %broadcast_in_dim.14), channel_id=1, replica_groups=mesh['z'=8,'x'=4,'c'=2,'yh'=4,'yl'=2] {'z','x'}, dimensions={0} | all-to-all | bytes 262144 | tf_op jit(solution)/shard_map/all_to_all | solution.py:302
  66.0 2.0 %first_rows.1 = (f32[1024,1024]{1,0:T(8,128)S(1)}, f32[8,128]{1,0:T(8,128)S(1)}, f32[8,128]{1,0:T(8,128)S(1)}) custom-call(f32[32,8,128]{2,1,0:T(8,128)S(1)} %all_to_all.45.refs_0_, f32[512,1024]{1,0:T(8,128)S(1)} %get-tuple-element.22.refs_1_, f32[512,1024]{1,0:T(8,128)S(1)} %get-tuple-element.23.refs_2_), custom_call_target="tpu_custom_call" | custom-call | tf_op jit(solution)/shard_map/first_rows/pallas_call | solution.py:338
  68.1 13.9 %all_to_all.46.refs_0_ = f32[16,8,128]{2,1,0:T(8,128)S(1)} all-to-all(f32[16,8,128]{2,1,0:T(8,128)S(1)} %broadcast_in_dim.15), channel_id=1, replica_groups=mesh['z'=8,'x'=4,'c'=2,'yh'=4,'yl'=2] {'yh','yl','c'}, dimensions={0} | all-to-all | bytes 131072 | tf_op jit(solution)/shard_map/all_to_all | solution.py:302
  82.0 0.6 first_cols.1
  82.6 11.9 %all_to_all.47.refs_0_ = bf16[32,8,128]{2,1,0:T(8,128)(2,1)S(1)} all-to-all(bf16[32,8,128]{2,1,0:T(8,128)(2,1)S(1)} %broadcast_in_dim.16), channel_id=1, replica_groups=mesh['z'=8,'x'=4,'c'=2,'yh'=4,'yl'=2] {'z','x'}, dimensions={0} | all-to-all | bytes 131072 | tf_op jit(solution)/shard_map/all_to_all | solution.py:302
  94.5 0.6 rows.2
  95.1 11.4 %all_to_all.48.refs_0_ = bf16[16,8,128]{2,1,0:T(8,128)(2,1)S(1)} all-to-all(bf16[16,8,128]{2,1,0:T(8,128)(2,1)S(1)} %broadcast_in_dim.17), channel_id=1, replica_groups=mesh['z'=8,'x'=4,'c'=2,'yh'=4,'yl'=2] {'yh','yl','c'}, dimensions={0} | all-to-all | bytes 65536 | tf_op jit(solution)/shard_map/all_to_all | solution.py:302
  106.6 0.6 cols.2
  107.2 11.8 %all_to_all.49.refs_0_ = bf16[32,8,128]{2,1,0:T(8,128)(2,1)S(1)} all-to-all(bf16[32,8,128]{2,1,0:T(8,128)(2,1)S(1)} %broadcast_in_dim.18), channel_id=1, replica_groups=mesh['z'=8,'x'=4,'c'=2,'yh'=4,'yl'=2] {'z','x'}, dimensions={0} | all-to-all | bytes 131072 | tf_op jit(solution)/shard_map/all_to_all | solution.py:302
  119.0 0.6 rows.3
  119.7 11.5 %all_to_all.50.refs_0_ = bf16[16,8,128]{2,1,0:T(8,128)(2,1)S(1)} all-to-all(bf16[16,8,128]{2,1,0:T(8,128)(2,1)S(1)} %broadcast_in_dim.19), channel_id=1, replica_groups=mesh['z'=8,'x'=4,'c'=2,'yh'=4,'yl'=2] {'yh','yl','c'}, dimensions={0} | all-to-all | bytes 65536 | tf_op jit(solution)/shard_map/all_to_all | solution.py:302
  131.2 0.6 cols.3
  131.8 11.8 %all_to_all.51.refs_0_ = bf16[32,8,128]{2,1,0:T(8,128)(2,1)S(1)} all-to-all(bf16[32,8,128]{2,1,0:T(8,128)(2,1)S(1)} %broadcast_in_dim.20), channel_id=1, replica_groups=mesh['z'=8,'x'=4,'c'=2,'yh'=4,'yl'=2] {'z','x'}, dimensions={0} | all-to-all | bytes 131072 | tf_op jit(solution)/shard_map/all_to_all | solution.py:302
  143.6 1.0 targets_far.1
  144.6 3.5 %collective-permute-start.2 = (bf16[8,72,512]{2,1,0:T(8,128)(2,1)S(1)}, bf16[8,72,512]{2,1,0:T(8,128)(2,1)S(1)}, u32[]{:S(2)}, u32[]{:S(2)}) collective-permute-start(bf16[8,72,512]{2,1,0:T(8,128)(2,1)S(1)} %targets_far.1), channel_id=1, source_target_pairs={{0,8},{8,0},{1,9},{9,1},{2,10},{10,2},{3,11},{11,3},{4,12},{12,4},... | collective-permute-start | bytes 1769480 | tf_op jit(solution)/shard_map/ppermute | solution.py:306
  148.2 1.0 targets_own.1
  149.2 0.6 collective-permute-done.2.far
  149.8 0.1 pack.1
  149.9 21.8 %all_to_all.52.parts = bf16[8,72,512]{2,1,0:T(8,128)(2,1)S(1)} all-to-all(bf16[8,72,512]{2,1,0:T(8,128)(2,1)S(1)} %pack.1), channel_id=1, replica_groups=mesh['z'=8,'x'=4,'c'=2,'yh'=4,'yl'=2] {'yh','yl'}, dimensions={0} | all-to-all | bytes 1179648 | tf_op jit(solution)/shard_map/all_to_all | solution.py:373
  171.7 0.7 finish.1
  (8 shorter events, 0.1 us)
Async XLA Ops:
  0.0 0.8 copy-start.1
  0.8 15.0 %copy-start = (bf16[512,64]{0,1:T(8,128)(2,1)S(1)}, bf16[512,64]{0,1:T(8,128)(2,1)}, u32[]{:S(2)}) copy-start(bf16[512,64]{0,1:T(8,128)(2,1)} %param.2) | copy-start | bytes 196612
  2.0 42.5 %all-to-all-start = ((bf16[32,32,512]{2,1,0:T(8,128)(2,1)}), bf16[32,32,512]{2,1,0:T(8,128)(2,1)S(1)}, u32[]{:S(2)}, u32[]{:S(2)}) async-start(bf16[32,32,512]{2,1,0:T(8,128)(2,1)} %spread.1), calls=%async_computation | async-start | bytes 2097152 | tf_op jit(solution)/shard_map/all_to_all | solution.py:323
  15.8 5.3 %collective-permute-start = (bf16[64,512]{1,0:T(8,128)(2,1)S(1)}, bf16[64,512]{1,0:T(8,128)(2,1)S(1)}, u32[]{:S(2)}, u32[]{:S(2)}) collective-permute-start(bf16[64,512]{1,0:T(8,128)(2,1)S(1)} %bitcast.7), channel_id=1, source_target_pairs={{0,1},{1,0},{2,3},{3,2},{4,5},{5,4},{6,7},{7,6},{8,9},{9,8},{10,11... | collective-permute-start | bytes 196616 | tf_op jit(solution)/shard_map/ppermute | solution.py:306
  38.5 7.6 %collective-permute-start.1 = (bf16[512,512]{1,0:T(8,128)(2,1)S(1)}, bf16[512,512]{1,0:T(8,128)(2,1)S(1)}, u32[]{:S(2)}, u32[]{:S(2)}) collective-permute-start(bf16[512,512]{1,0:T(8,128)(2,1)S(1)} %noise.1), channel_id=1, source_target_pairs={{0,8},{8,0},{1,9},{9,1},{2,10},{10,2},{3,11},{11,3},{4,12},{12,4},... | collective-permute-start | bytes 1572872 | tf_op jit(solution)/shard_map/ppermute | solution.py:306
  144.6 5.2 %collective-permute-start.2 = (bf16[8,72,512]{2,1,0:T(8,128)(2,1)S(1)}, bf16[8,72,512]{2,1,0:T(8,128)(2,1)S(1)}, u32[]{:S(2)}, u32[]{:S(2)}) collective-permute-start(bf16[8,72,512]{2,1,0:T(8,128)(2,1)S(1)} %targets_far.1), channel_id=1, source_target_pairs={{0,8},{8,0},{1,9},{9,1},{2,10},{10,2},{3,11},{11,3},{4,12},{12,4},... | collective-permute-start | bytes 1769480 | tf_op jit(solution)/shard_map/ppermute | solution.py:306

commit v7 on v6

--- a/solution.py
+++ b/solution.py
@@ -38,17 +38,33 @@
     )
 
 
+def three(val):
+    high = val.astype(BF16).astype(F32)
+    mid = (val - high).astype(BF16).astype(F32)
+    return high, mid, val - high - mid
+
+
 def lanes_to_rows(vec, out_ref):
+    square = (128, 128)
+    on_diagonal = lax.broadcasted_iota(jnp.int32, square, 0) == lax.broadcasted_iota(jnp.int32, square, 1)
+    ones = jnp.ones((3 * 128, 128), BF16)
     for r in range(vec.shape[0]):
-        block = jnp.broadcast_to(vec[r : r + 1, :], (128, 128))
-        out_ref[r * 128 : (r + 1) * 128, :] = block.T
+        pieces = [
+            jnp.where(on_diagonal, jnp.broadcast_to(piece, square), 0.0).astype(BF16)
+            for piece in three(vec[r : r + 1, :])
+        ]
+        out_ref[r * 128 : (r + 1) * 128, :] = jnp.dot(
+            jnp.concatenate(pieces, axis=1), ones, preferred_element_type=F32
+        )
 
 
 def rows_to_lanes(ref):
-    parts = []
-    for r in range(ref.shape[0] // 128):
-        parts.append(jnp.sum(ref[r * 128 : (r + 1) * 128, :].T, axis=0, keepdims=True))
-    return jnp.concatenate(parts, axis=0)
+    ones = jnp.ones((8, 3 * 128), BF16)
+    pieces = jnp.concatenate([piece.astype(BF16) for piece in three(ref[...])], axis=1)
+    sums = lax.dot_general(ones, pieces, (((1,), (1,)), ((), ())), preferred_element_type=F32)
+    return jnp.concatenate(
+        [sums[0:1, r * 128 : (r + 1) * 128] for r in range(ref.shape[0] // 128)], axis=0
+    )
 
 
 def flat(vec):

time: 173 us -> 174 us (level)
  no operation moved by 1% of the time
where the time goes in v7:
time: 174 us; the launch traced here: 173 us
  blocking collectives  130 us (75%)
  starting transfers between devices  26.6 us (15%)
  Pallas kernels  13.3 us (8%)
  waiting for transfers between devices  2.83 us (2%)
    all_to_all x7, blocking collectives, everyone(): return lax.all_to_all(copies, axes, 0, 0, tiled=True)  91.1 us
    all_to_all x1, blocking collectives, on_device(): got = lax.all_to_all(pieces, COL, 0, 0, tiled=True)  21.8 us
    all_gather x1, blocking collectives, on_device(): lax.all_gather(pair, 'yh', axis=0).reshape(cols_all, slice_width, half)  16.9 us
    all_to_all x1, starting transfers between devices, on_device(): lax.all_to_all(copies, row_axes, 0, 0, tiled=True).reshape(wide, depth)  13.7 us
    ppermute x3, starting transfers between devices, swapped(): return lax.ppermute(val, axis, [(0, 1), (1, 0)])  12.8 us
  transfers between devices with their start and end apart: 4, of which 3 were waited for; matrix products, arithmetic and copies ran while one was open for 0% of the time, Pallas kernels for 2%

profile of v7, /device:TPU:1, one launch (start us, length us, event | category | flops | bytes accessed | tf_op | source)
XLA Modules:
  0.0 173.4 jit_solution(11726581603209758495)
XLA Ops:
  0.0 0.0 copy-start.1
  0.0 0.8 copy-done.1
  0.8 0.0 copy-start
  0.8 1.3 spread.1
  2.0 13.7 %all-to-all-start = ((bf16[32,32,512]{2,1,0:T(8,128)(2,1)}), bf16[32,32,512]{2,1,0:T(8,128)(2,1)S(1)}, u32[]{:S(2)}, u32[]{:S(2)}) async-start(bf16[32,32,512]{2,1,0:T(8,128)(2,1)} %spread.1), calls=%async_computation | async-start | bytes 2097152 | tf_op jit(solution)/shard_map/all_to_all | solution.py:339
  15.8 0.0 copy-done
  15.8 3.2 %collective-permute-start = (bf16[64,512]{1,0:T(8,128)(2,1)S(1)}, bf16[64,512]{1,0:T(8,128)(2,1)S(1)}, u32[]{:S(2)}, u32[]{:S(2)}) collective-permute-start(bf16[64,512]{1,0:T(8,128)(2,1)S(1)} %bitcast.7), channel_id=1, source_target_pairs={{0,1},{1,0},{2,3},{3,2},{4,5},{5,4},{6,7},{7,6},{8,9},{9,8},{10,11... | collective-permute-start | bytes 196616 | tf_op jit(solution)/shard_map/ppermute | solution.py:322
  19.0 2.1 %collective-permute-done.there = bf16[64,512]{1,0:T(8,128)(2,1)S(1)} collective-permute-done((bf16[64,512]{1,0:T(8,128)(2,1)S(1)}, bf16[64,512]{1,0:T(8,128)(2,1)S(1)}, u32[]{:S(2)}, u32[]{:S(2)}) %collective-permute-start) | collective-permute-done | bytes 65568 | tf_op jit(solution)/shard_map/ppermute | solution.py:322
  21.1 16.9 %all-gather.parts = bf16[8,64,512]{2,1,0:T(8,128)(2,1)S(1)} all-gather(bf16[2,64,512]{2,1,0:T(8,128)(2,1)S(1)} %pair.1), channel_id=2, replica_groups=mesh['z'=8,'x'=4,'c'=2,'yh'=4,'yl'=2] {'yh'}, dimensions={0}, use_global_device_ids=true | all-gather | bytes 655360 | tf_op jit(solution)/shard_map/all_gather | solution.py:337
  38.0 0.5 noise.1
  38.5 6.1 %collective-permute-start.1 = (bf16[512,512]{1,0:T(8,128)(2,1)S(1)}, bf16[512,512]{1,0:T(8,128)(2,1)S(1)}, u32[]{:S(2)}, u32[]{:S(2)}) collective-permute-start(bf16[512,512]{1,0:T(8,128)(2,1)S(1)} %noise.1), channel_id=1, source_target_pairs={{0,8},{8,0},{1,9},{9,1},{2,10},{10,2},{3,11},{11,3},{4,12},{12,4},... | collective-permute-start | bytes 1572872 | tf_op jit(solution)/shard_map/ppermute | solution.py:322
  44.6 0.0 all-to-all-done
  44.6 1.3 cost_own.1
  45.8 0.3 collective-permute-done.1.noise
  46.1 1.2 cost_far.1
  47.3 18.7 %all_to_all.45.refs_0_ = f32[32,8,128]{2,1,0:T(8,128)S(1)} all-to-all(f32[32,8,128]{2,1,0:T(8,128)S(1)} %broadcast_in_dim.14), channel_id=1, replica_groups=mesh['z'=8,'x'=4,'c'=2,'yh'=4,'yl'=2] {'z','x'}, dimensions={0} | all-to-all | bytes 262144 | tf_op jit(solution)/shard_map/all_to_all | solution.py:318
  66.0 2.3 %first_rows.1 = (f32[1024,1024]{1,0:T(8,128)S(1)}, f32[8,128]{1,0:T(8,128)S(1)}, f32[8,128]{1,0:T(8,128)S(1)}) custom-call(f32[32,8,128]{2,1,0:T(8,128)S(1)} %all_to_all.45.refs_0_, f32[512,1024]{1,0:T(8,128)S(1)} %get-tuple-element.22.refs_1_, f32[512,1024]{1,0:T(8,128)S(1)} %get-tuple-element.23.refs_2_), custom_call_target="tpu_custom_call" | custom-call | tf_op jit(solution)/shard_map/first_rows/pallas_call | solution.py:354
  68.3 13.9 %all_to_all.46.refs_0_ = f32[16,8,128]{2,1,0:T(8,128)S(1)} all-to-all(f32[16,8,128]{2,1,0:T(8,128)S(1)} %broadcast_in_dim.15), channel_id=1, replica_groups=mesh['z'=8,'x'=4,'c'=2,'yh'=4,'yl'=2] {'yh','yl','c'}, dimensions={0} | all-to-all | bytes 131072 | tf_op jit(solution)/shard_map/all_to_all | solution.py:318
  82.2 0.8 first_cols.1
  83.0 11.9 %all_to_all.47.refs_0_ = bf16[32,8,128]{2,1,0:T(8,128)(2,1)S(1)} all-to-all(bf16[32,8,128]{2,1,0:T(8,128)(2,1)S(1)} %broadcast_in_dim.16), channel_id=1, replica_groups=mesh['z'=8,'x'=4,'c'=2,'yh'=4,'yl'=2] {'z','x'}, dimensions={0} | all-to-all | bytes 131072 | tf_op jit(solution)/shard_map/all_to_all | solution.py:318
  94.9 0.7 rows.2
  95.6 11.4 %all_to_all.48.refs_0_ = bf16[16,8,128]{2,1,0:T(8,128)(2,1)S(1)} all-to-all(bf16[16,8,128]{2,1,0:T(8,128)(2,1)S(1)} %broadcast_in_dim.17), channel_id=1, replica_groups=mesh['z'=8,'x'=4,'c'=2,'yh'=4,'yl'=2] {'yh','yl','c'}, dimensions={0} | all-to-all | bytes 65536 | tf_op jit(solution)/shard_map/all_to_all | solution.py:318
  107.1 0.7 cols.2
  107.8 11.8 %all_to_all.49.refs_0_ = bf16[32,8,128]{2,1,0:T(8,128)(2,1)S(1)} all-to-all(bf16[32,8,128]{2,1,0:T(8,128)(2,1)S(1)} %broadcast_in_dim.18), channel_id=1, replica_groups=mesh['z'=8,'x'=4,'c'=2,'yh'=4,'yl'=2] {'z','x'}, dimensions={0} | all-to-all | bytes 131072 | tf_op jit(solution)/shard_map/all_to_all | solution.py:318
  119.7 0.7 rows.3
  120.4 11.5 %all_to_all.50.refs_0_ = bf16[16,8,128]{2,1,0:T(8,128)(2,1)S(1)} all-to-all(bf16[16,8,128]{2,1,0:T(8,128)(2,1)S(1)} %broadcast_in_dim.19), channel_id=1, replica_groups=mesh['z'=8,'x'=4,'c'=2,'yh'=4,'yl'=2] {'yh','yl','c'}, dimensions={0} | all-to-all | bytes 65536 | tf_op jit(solution)/shard_map/all_to_all | solution.py:318
  131.9 0.7 cols.3
  132.7 11.8 %all_to_all.51.refs_0_ = bf16[32,8,128]{2,1,0:T(8,128)(2,1)S(1)} all-to-all(bf16[32,8,128]{2,1,0:T(8,128)(2,1)S(1)} %broadcast_in_dim.20), channel_id=1, replica_groups=mesh['z'=8,'x'=4,'c'=2,'yh'=4,'yl'=2] {'z','x'}, dimensions={0} | all-to-all | bytes 131072 | tf_op jit(solution)/shard_map/all_to_all | solution.py:318
  144.5 1.1 targets_far.1
  145.6 3.5 %collective-permute-start.2 = (bf16[8,72,512]{2,1,0:T(8,128)(2,1)S(1)}, bf16[8,72,512]{2,1,0:T(8,128)(2,1)S(1)}, u32[]{:S(2)}, u32[]{:S(2)}) collective-permute-start(bf16[8,72,512]{2,1,0:T(8,128)(2,1)S(1)} %targets_far.1), channel_id=1, source_target_pairs={{0,8},{8,0},{1,9},{9,1},{2,10},{10,2},{3,11},{11,3},{4,12},{12,4},... | collective-permute-start | bytes 1769480 | tf_op jit(solution)/shard_map/ppermute | solution.py:322
  149.2 1.1 targets_own.1
  150.3 0.5 collective-permute-done.2.far
  150.8 0.1 pack.1
  150.9 21.8 %all_to_all.52.parts = bf16[8,72,512]{2,1,0:T(8,128)(2,1)S(1)} all-to-all(bf16[8,72,512]{2,1,0:T(8,128)(2,1)S(1)} %pack.1), channel_id=1, replica_groups=mesh['z'=8,'x'=4,'c'=2,'yh'=4,'yl'=2] {'yh','yl'}, dimensions={0} | all-to-all | bytes 1179648 | tf_op jit(solution)/shard_map/all_to_all | solution.py:389
  172.7 0.7 finish.1
  (8 shorter events, 0.1 us)
Async XLA Ops:
  0.0 0.8 copy-start.1
  0.8 15.0 %copy-start = (bf16[512,64]{0,1:T(8,128)(2,1)S(1)}, bf16[512,64]{0,1:T(8,128)(2,1)}, u32[]{:S(2)}) copy-start(bf16[512,64]{0,1:T(8,128)(2,1)} %param.2) | copy-start | bytes 196612
  2.0 42.5 %all-to-all-start = ((bf16[32,32,512]{2,1,0:T(8,128)(2,1)}), bf16[32,32,512]{2,1,0:T(8,128)(2,1)S(1)}, u32[]{:S(2)}, u32[]{:S(2)}) async-start(bf16[32,32,512]{2,1,0:T(8,128)(2,1)} %spread.1), calls=%async_computation | async-start | bytes 2097152 | tf_op jit(solution)/shard_map/all_to_all | solution.py:339
  15.8 5.3 %collective-permute-start = (bf16[64,512]{1,0:T(8,128)(2,1)S(1)}, bf16[64,512]{1,0:T(8,128)(2,1)S(1)}, u32[]{:S(2)}, u32[]{:S(2)}) collective-permute-start(bf16[64,512]{1,0:T(8,128)(2,1)S(1)} %bitcast.7), channel_id=1, source_target_pairs={{0,1},{1,0},{2,3},{3,2},{4,5},{5,4},{6,7},{7,6},{8,9},{9,8},{10,11... | collective-permute-start | bytes 196616 | tf_op jit(solution)/shard_map/ppermute | solution.py:322
  38.5 7.6 %collective-permute-start.1 = (bf16[512,512]{1,0:T(8,128)(2,1)S(1)}, bf16[512,512]{1,0:T(8,128)(2,1)S(1)}, u32[]{:S(2)}, u32[]{:S(2)}) collective-permute-start(bf16[512,512]{1,0:T(8,128)(2,1)S(1)} %noise.1), channel_id=1, source_target_pairs={{0,8},{8,0},{1,9},{9,1},{2,10},{10,2},{3,11},{11,3},{4,12},{12,4},... | collective-permute-start | bytes 1572872 | tf_op jit(solution)/shard_map/ppermute | solution.py:322
  145.6 5.2 %collective-permute-start.2 = (bf16[8,72,512]{2,1,0:T(8,128)(2,1)S(1)}, bf16[8,72,512]{2,1,0:T(8,128)(2,1)S(1)}, u32[]{:S(2)}, u32[]{:S(2)}) collective-permute-start(bf16[8,72,512]{2,1,0:T(8,128)(2,1)S(1)} %targets_far.1), channel_id=1, source_target_pairs={{0,8},{8,0},{1,9},{9,1},{2,10},{10,2},{3,11},{11,3},{4,12},{12,4},... | collective-permute-start | bytes 1769480 | tf_op jit(solution)/shard_map/ppermute | solution.py:322

commit v8 on v6

--- a/solution.py
+++ b/solution.py
@@ -129,7 +129,7 @@
 
 
 def first_row_body(log_data, n, *refs):
-    parts, (own, far, expd, peak, lse, part, tops) = refs[:n], refs[n:]
+    parts, (own, far, expd, tops, lse, part) = refs[:n], refs[n:]
     rows, cols = expd.shape
     half = own.shape[0]
     pot = jnp.broadcast_to(flat(-log_data - merged(parts)), (8, cols))
@@ -140,40 +140,28 @@
     for flip, score in enumerate((own, far)):
         base = half_at(flip, half)
 
-        def find(r, carry):
+        def body(r, carry):
+            at = rows_at(base, r)
             val = score[rows_at(0, r), :] + pot
-            part[rows_at(base, r), :] = functools.reduce(
-                jnp.maximum, [val[:, t * 128 : (t + 1) * 128] for t in range(cols // 128)]
-            )
-            return carry
-
-        lax.fori_loop(0, half // 8, find, 0, unroll=8)
-    high = jnp.concatenate(
-        [
-            jnp.max(part[r * 128 : (r + 1) * 128, :].T, axis=0, keepdims=True)
-            for r in range(rows // 128)
-        ],
-        axis=0,
-    )
-    lanes_to_rows(high - SHIFT, tops)
-    for flip, score in enumerate((own, far)):
-        base = half_at(flip, half)
-
-        def raise_up(r, carry):
-            at = rows_at(base, r)
-            top = jnp.concatenate([tops[at, :]] * (cols // 128), axis=1)
-            e = jnp.exp2((score[rows_at(0, r), :] + pot) - top)
+            tiles = [val[:, t * 128 : (t + 1) * 128] for t in range(cols // 128)]
+            top = functools.reduce(jnp.maximum, tiles)
+            tops[at, :] = top
+            low = top - SHIFT
+            e = jnp.concatenate([jnp.exp2(tile - low) for tile in tiles], axis=1)
             expd[at, :] = e
             part[at, :] = lane_sum(e)
             return carry
 
-        lax.fori_loop(0, half // 8, raise_up, 0, unroll=8)
-    peak[...] = high
-    lse[...] = high + (jnp.log2(rows_to_lanes(part)) - SHIFT)
-
-
-def column_sums(expd, factor, factors, out):
-    lanes_to_rows(factor, factors)
+        lax.fori_loop(0, half // 8, body, 0, unroll=8)
+    for r in range(rows // 128):
+        at = slice(r * 128, (r + 1) * 128)
+        turned = tops[at, :].T
+        high = jnp.max(turned, axis=0, keepdims=True)
+        total = jnp.sum(jnp.exp2(turned - high) * part[at, :].T, axis=0, keepdims=True)
+        lse[r : r + 1, :] = high + (jnp.log2(total) - SHIFT)
+
+
+def column_sums(expd, factors, out, rows_out):
     rows, cols = expd.shape
     copies = cols // 128
 
@@ -185,25 +173,25 @@
     acc = lax.fori_loop(0, rows // 8, body, jnp.zeros((8, cols), F32), unroll=8)
     sums = jnp.sum(acc, axis=0, keepdims=True)
     count, width = out.shape
-    rows_out = factors.at[0:count, :]
     for t in range(count):
         rows_out[t : t + 1, :] = sums[:, t * width : (t + 1) * width]
     out[...] = rows_out[...].astype(out.dtype)
 
 
 def first_col_body(count, n, *refs):
-    parts, (peak, expd, out, scale, factors) = refs[:n], refs[n:]
-    s = jnp.exp2(peak[...] - merged(parts) + SHIFT)
+    parts, (tops, expd, out, scale, factors, rows_out) = refs[:n], refs[n:]
+    lanes_to_rows(merged(parts) - SHIFT, factors)
+    s = jnp.exp2(tops[...] - factors[...])
     scale[...] = s
-    column_sums(expd, s * (1.0 / count), factors, out)
+    factors[...] = s * (1.0 / count)
+    column_sums(expd, factors, out, rows_out)
 
 
 def col_body(count, n, *refs):
-    parts, (scale, expd, out, *factor, factors) = refs[:n], refs[n:]
-    f = scale[...] * ((SCALE / count) / added(parts))
-    for ref in factor:
-        ref[...] = f
-    column_sums(expd, f, factors, out)
+    parts, (scale, expd, out, factors, rows_out) = refs[:n], refs[n:]
+    lanes_to_rows((SCALE / count) / added(parts), factors)
+    factors[...] = factors[...] * scale[...]
+    column_sums(expd, factors, out, rows_out)
 
 
 def row_body(count, n, *refs):
@@ -213,11 +201,11 @@
 
     def body(r, carry):
         at = pl.ds(pl.multiple_of(r * 8, 8), 8)
-        part[at, :] = lane_sum(expd[at, :] * v)
+        part[at, :] = lane_sum(expd[at, :] * v) * scale[at, :]
         return carry
 
     lax.fori_loop(0, rows // 8, body, 0, unroll=8)
-    out[...] = (rows_to_lanes(part) * scale[...]).astype(out.dtype)
+    out[...] = rows_to_lanes(part).astype(out.dtype)
 
 
 def split_three(mass, deep):
@@ -233,18 +221,17 @@
 
 def target_body(count, flip, n, *refs):
     parts, (factor, expd, data, out) = refs[:n], refs[n : n + 4]
-    *mass, part, factors = refs[n + 4 :]
+    *mass, part = refs[n + 4 :]
     v = jnp.broadcast_to(flat((SCALE / count) / added(parts)), (128, expd.shape[1]))
-    half, wide = factors.shape[0], expd.shape[1]
+    half, wide = expd.shape[0] // 2, expd.shape[1]
     base = half_at(flip, half)
-    first = lax.rem(lax.axis_index("c") + flip, 2) * (half // 128)
-    lanes_to_rows(factor[pl.ds(first, half // 128), :], factors)
     cols, deep, _ = out.shape
     depth = data.shape[1] // cols
     for r in range(half // 128):
         at = slice(r * 128, (r + 1) * 128)
-        f = jnp.concatenate([factors[at, :]] * (wide // 128), axis=1)
-        w = expd[pl.ds(pl.multiple_of(base + r * 128, 128), 128), :] * v * f
+        rows_here = pl.ds(pl.multiple_of(base + r * 128, 128), 128)
+        f = jnp.concatenate([factor[rows_here, :]] * (wide // 128), axis=1)
+        w = expd[rows_here, :] * v * f
         total = jnp.sum(lane_sum(w).T, axis=0, keepdims=True)
         part[r : r + 1, :] = total
         block = jnp.dot(w.astype(BF16), data[...], preferred_element_type=F32).T
@@ -276,24 +263,9 @@
     out[1 - place] = there[...]
 
 
-def spread_body(val, out, sems):
-    copies = [pltpu.make_async_copy(val, out.at[k], sems.at[k]) for k in range(out.shape[0])]
-    for copy in copies:
-        copy.start()
-    for copy in copies:
-        copy.wait()
-
-
-def spread(val, count):
-    return pl.pallas_call(
-        spread_body,
-        out_shape=jax.ShapeDtypeStruct((count,) + val.shape, val.dtype),
-        in_specs=[VM],
-        out_specs=pl.BlockSpec(memory_space=pl.ANY),
-        scratch_shapes=[pltpu.SemaphoreType.DMA((count,))],
-        compiler_params=params(32),
-        name="spread",
-    )(val)
+def spread_body(val, out):
+    for k in range(out.shape[0]):
+        out[k] = val[...]
 
 
 def everyone(val, axes):
@@ -319,7 +291,7 @@
     here = noise.T
     pair = call(pair_body, jax.ShapeDtypeStruct((2,) + here.shape, BF16), 2, name="pair")(here, swapped(here, "yl"))
     noise_parts = lax.all_gather(pair, "yh", axis=0).reshape(cols_all, slice_width, half)
-    copies = spread(data, zs * xs)
+    copies = call(spread_body, vmem((zs * xs,) + data.shape, BF16), 1, name="spread")(data)
     data_all = lax.all_to_all(copies, row_axes, 0, 0, tiled=True).reshape(wide, depth)
     own = call(noise_body, jax.ShapeDtypeStruct((half, depth), BF16), 1, name="noise")(noise_parts)
     far = swapped(own)
@@ -335,15 +307,17 @@
     score_own, *before = call(cost_body, cost_outs, 2, cost_scratch, name="cost_own")(own, data_all)
     score_far, lse, _ = call(cost_body, cost_outs, 4, cost_scratch, name="cost_far")(far, data_all, *before)
     parts = everyone(lse, row_axes)
-    expd, peak, lse = call(
+    by_lane = jax.ShapeDtypeStruct((rows, 128), F32)
+    small = pltpu.VMEM((wide // 128, 128), F32)
+    expd, tops, lse = call(
         functools.partial(first_row_body, log_data, 1),
-        (vmem((rows, wide), F32), vec_row, vec_row), 3, [strip, strip], name="first_rows",
+        (vmem((rows, wide), F32), by_lane, vec_row), 3, [strip], name="first_rows",
     )(parts, score_own, score_far)
     parts = everyone(lse, col_axes)
     sums, scale = call(
         functools.partial(first_col_body, count_noise, 1),
-        (sent_col, vec_row), 3, [strip], name="first_cols",
-    )(parts, peak, expd)
+        (sent_col, by_lane), 3, [strip, small], name="first_cols",
+    )(parts, tops, expd)
     for sweep in range(1, ITERS - 1):
         parts = everyone(sums, row_axes)
         mass = call(
@@ -353,12 +327,13 @@
         last = sweep == ITERS - 2
         sums, *factor = call(
             functools.partial(col_body, count_noise, 1),
-            (sent_col, vec_row) if last else (sent_col,), 3, [strip], name="cols",
+            (sent_col, by_lane) if last else (sent_col,),
+            3, [small] if last else [strip, small], name="cols",
         )(parts, scale, expd)
     (factor,) = factor
     parts = everyone(sums, row_axes)
 
-    strips = [pltpu.VMEM((half // 128, 128), F32), pltpu.VMEM((half, 128), F32)]
+    strips = [pltpu.VMEM((half // 128, 128), F32)]
     packed = jax.ShapeDtypeStruct((cols_all, slice_width + 8, half), BF16)
     far = call(
         functools.partial(target_body, count_data, 1, 1), packed, 4, strips, name="targets_far"

time: 173 us -> 172 us (level)
  no operation moved by 1% of the time
where the time goes in v8:
time: 172 us
  blocking collectives  130 us (76%)
  starting transfers between devices  26.6 us (15%)
  Pallas kernels  11.3 us (7%)
  waiting for transfers between devices  3.07 us (2%)
    all_to_all x7, blocking collectives, everyone(): return lax.all_to_all(copies, axes, 0, 0, tiled=True)  91.1 us
    all_to_all x1, blocking collectives, on_device(): got = lax.all_to_all(pieces, COL, 0, 0, tiled=True)  21.8 us
    all_gather x1, blocking collectives, on_device(): lax.all_gather(pair, 'yh', axis=0).reshape(cols_all, slice_width, half)  16.9 us
    all_to_all x1, starting transfers between devices, on_device(): lax.all_to_all(copies, row_axes, 0, 0, tiled=True).reshape(wide, depth)  13.7 us
    ppermute x3, starting transfers between devices, swapped(): return lax.ppermute(val, axis, [(0, 1), (1, 0)])  12.8 us
  transfers between devices with their start and end apart: 4, of which 3 were waited for; matrix products, arithmetic and copies ran while one was open for 0% of the time, Pallas kernels for 2%

profile of v8, /device:TPU:1, one launch (start us, length us, event | category | flops | bytes accessed | tf_op | source)
XLA Modules:
  0.0 171.6 jit_solution(14230349320944090636)
XLA Ops:
  0.0 0.0 copy-start.1
  0.0 0.8 copy-done.1
  0.8 0.0 copy-start
  0.8 1.0 spread.1
  1.8 13.7 %all-to-all-start = ((bf16[32,32,512]{2,1,0:T(8,128)(2,1)}), bf16[32,32,512]{2,1,0:T(8,128)(2,1)S(1)}, u32[]{:S(2)}, u32[]{:S(2)}) async-start(bf16[32,32,512]{2,1,0:T(8,128)(2,1)} %spread.1), calls=%async_computation | async-start | bytes 2097152 | tf_op jit(solution)/shard_map/all_to_all | solution.py:295
  15.5 0.0 copy-done
  15.5 3.2 %collective-permute-start = (bf16[64,512]{1,0:T(8,128)(2,1)S(1)}, bf16[64,512]{1,0:T(8,128)(2,1)S(1)}, u32[]{:S(2)}, u32[]{:S(2)}) collective-permute-start(bf16[64,512]{1,0:T(8,128)(2,1)S(1)} %bitcast.7), channel_id=1, source_target_pairs={{0,1},{1,0},{2,3},{3,2},{4,5},{5,4},{6,7},{7,6},{8,9},{9,8},{10,11... | collective-permute-start | bytes 196616 | tf_op jit(solution)/shard_map/ppermute | solution.py:278
  18.7 2.1 %collective-permute-done.there = bf16[64,512]{1,0:T(8,128)(2,1)S(1)} collective-permute-done((bf16[64,512]{1,0:T(8,128)(2,1)S(1)}, bf16[64,512]{1,0:T(8,128)(2,1)S(1)}, u32[]{:S(2)}, u32[]{:S(2)}) %collective-permute-start) | collective-permute-done | bytes 65568 | tf_op jit(solution)/shard_map/ppermute | solution.py:278
  20.9 16.9 %all-gather.parts = bf16[8,64,512]{2,1,0:T(8,128)(2,1)S(1)} all-gather(bf16[2,64,512]{2,1,0:T(8,128)(2,1)S(1)} %pair.1), channel_id=2, replica_groups=mesh['z'=8,'x'=4,'c'=2,'yh'=4,'yl'=2] {'yh'}, dimensions={0}, use_global_device_ids=true | all-gather | bytes 655360 | tf_op jit(solution)/shard_map/all_gather | solution.py:293
  37.7 0.5 noise.1
  38.2 6.1 %collective-permute-start.1 = (bf16[512,512]{1,0:T(8,128)(2,1)S(1)}, bf16[512,512]{1,0:T(8,128)(2,1)S(1)}, u32[]{:S(2)}, u32[]{:S(2)}) collective-permute-start(bf16[512,512]{1,0:T(8,128)(2,1)S(1)} %noise.1), channel_id=1, source_target_pairs={{0,8},{8,0},{1,9},{9,1},{2,10},{10,2},{3,11},{11,3},{4,12},{12,4},... | collective-permute-start | bytes 1572872 | tf_op jit(solution)/shard_map/ppermute | solution.py:278
  44.3 0.0 all-to-all-done
  44.3 1.1 cost_own.1
  45.4 0.4 collective-permute-done.1.noise
  45.8 1.2 cost_far.1
  47.1 18.7 %all_to_all.45.refs_0_ = f32[32,8,128]{2,1,0:T(8,128)S(1)} all-to-all(f32[32,8,128]{2,1,0:T(8,128)S(1)} %broadcast_in_dim.14), channel_id=1, replica_groups=mesh['z'=8,'x'=4,'c'=2,'yh'=4,'yl'=2] {'z','x'}, dimensions={0} | all-to-all | bytes 262144 | tf_op jit(solution)/shard_map/all_to_all | solution.py:274
  65.8 1.5 first_rows.1
  67.3 13.9 %all_to_all.46.refs_0_ = f32[16,8,128]{2,1,0:T(8,128)S(1)} all-to-all(f32[16,8,128]{2,1,0:T(8,128)S(1)} %broadcast_in_dim.15), channel_id=1, replica_groups=mesh['z'=8,'x'=4,'c'=2,'yh'=4,'yl'=2] {'yh','yl','c'}, dimensions={0} | all-to-all | bytes 131072 | tf_op jit(solution)/shard_map/all_to_all | solution.py:274
  81.2 0.6 first_cols.1
  81.8 11.9 %all_to_all.47.refs_0_ = bf16[32,8,128]{2,1,0:T(8,128)(2,1)S(1)} all-to-all(bf16[32,8,128]{2,1,0:T(8,128)(2,1)S(1)} %broadcast_in_dim.16), channel_id=1, replica_groups=mesh['z'=8,'x'=4,'c'=2,'yh'=4,'yl'=2] {'z','x'}, dimensions={0} | all-to-all | bytes 131072 | tf_op jit(solution)/shard_map/all_to_all | solution.py:274
  93.7 0.6 rows.2
  94.4 11.4 %all_to_all.48.refs_0_ = bf16[16,8,128]{2,1,0:T(8,128)(2,1)S(1)} all-to-all(bf16[16,8,128]{2,1,0:T(8,128)(2,1)S(1)} %broadcast_in_dim.17), channel_id=1, replica_groups=mesh['z'=8,'x'=4,'c'=2,'yh'=4,'yl'=2] {'yh','yl','c'}, dimensions={0} | all-to-all | bytes 65536 | tf_op jit(solution)/shard_map/all_to_all | solution.py:274
  105.8 0.6 cols.2
  106.4 11.8 %all_to_all.49.refs_0_ = bf16[32,8,128]{2,1,0:T(8,128)(2,1)S(1)} all-to-all(bf16[32,8,128]{2,1,0:T(8,128)(2,1)S(1)} %broadcast_in_dim.18), channel_id=1, replica_groups=mesh['z'=8,'x'=4,'c'=2,'yh'=4,'yl'=2] {'z','x'}, dimensions={0} | all-to-all | bytes 131072 | tf_op jit(solution)/shard_map/all_to_all | solution.py:274
  118.2 0.6 rows.3
  118.9 11.5 %all_to_all.50.refs_0_ = bf16[16,8,128]{2,1,0:T(8,128)(2,1)S(1)} all-to-all(bf16[16,8,128]{2,1,0:T(8,128)(2,1)S(1)} %broadcast_in_dim.19), channel_id=1, replica_groups=mesh['z'=8,'x'=4,'c'=2,'yh'=4,'yl'=2] {'yh','yl','c'}, dimensions={0} | all-to-all | bytes 65536 | tf_op jit(solution)/shard_map/all_to_all | solution.py:274
  130.4 0.6 cols.3
  131.0 11.8 %all_to_all.51.refs_0_ = bf16[32,8,128]{2,1,0:T(8,128)(2,1)S(1)} all-to-all(bf16[32,8,128]{2,1,0:T(8,128)(2,1)S(1)} %broadcast_in_dim.20), channel_id=1, replica_groups=mesh['z'=8,'x'=4,'c'=2,'yh'=4,'yl'=2] {'z','x'}, dimensions={0} | all-to-all | bytes 131072 | tf_op jit(solution)/shard_map/all_to_all | solution.py:274
  142.8 1.0 targets_far.1
  143.8 3.5 %collective-permute-start.2 = (bf16[8,72,512]{2,1,0:T(8,128)(2,1)S(1)}, bf16[8,72,512]{2,1,0:T(8,128)(2,1)S(1)}, u32[]{:S(2)}, u32[]{:S(2)}) collective-permute-start(bf16[8,72,512]{2,1,0:T(8,128)(2,1)S(1)} %targets_far.1), channel_id=1, source_target_pairs={{0,8},{8,0},{1,9},{9,1},{2,10},{10,2},{3,11},{11,3},{4,12},{12,4},... | collective-permute-start | bytes 1769480 | tf_op jit(solution)/shard_map/ppermute | solution.py:278
  147.4 1.0 targets_own.1
  148.4 0.6 collective-permute-done.2.far
  149.0 0.1 pack.1
  149.1 21.8 %all_to_all.52.parts = bf16[8,72,512]{2,1,0:T(8,128)(2,1)S(1)} all-to-all(bf16[8,72,512]{2,1,0:T(8,128)(2,1)S(1)} %pack.1), channel_id=1, replica_groups=mesh['z'=8,'x'=4,'c'=2,'yh'=4,'yl'=2] {'yh','yl'}, dimensions={0} | all-to-all | bytes 1179648 | tf_op jit(solution)/shard_map/all_to_all | solution.py:348
  170.9 0.7 finish.1
  (8 shorter events, 0.1 us)
Async XLA Ops:
  0.0 0.8 copy-start.1
  0.8 14.8 %copy-start = (bf16[512,64]{0,1:T(8,128)(2,1)S(1)}, bf16[512,64]{0,1:T(8,128)(2,1)}, u32[]{:S(2)}) copy-start(bf16[512,64]{0,1:T(8,128)(2,1)} %param.2) | copy-start | bytes 196612
  1.8 42.5 %all-to-all-start = ((bf16[32,32,512]{2,1,0:T(8,128)(2,1)}), bf16[32,32,512]{2,1,0:T(8,128)(2,1)S(1)}, u32[]{:S(2)}, u32[]{:S(2)}) async-start(bf16[32,32,512]{2,1,0:T(8,128)(2,1)} %spread.1), calls=%async_computation | async-start | bytes 2097152 | tf_op jit(solution)/shard_map/all_to_all | solution.py:295
  15.5 5.3 %collective-permute-start = (bf16[64,512]{1,0:T(8,128)(2,1)S(1)}, bf16[64,512]{1,0:T(8,128)(2,1)S(1)}, u32[]{:S(2)}, u32[]{:S(2)}) collective-permute-start(bf16[64,512]{1,0:T(8,128)(2,1)S(1)} %bitcast.7), channel_id=1, source_target_pairs={{0,1},{1,0},{2,3},{3,2},{4,5},{5,4},{6,7},{7,6},{8,9},{9,8},{10,11... | collective-permute-start | bytes 196616 | tf_op jit(solution)/shard_map/ppermute | solution.py:278
  38.2 7.6 %collective-permute-start.1 = (bf16[512,512]{1,0:T(8,128)(2,1)S(1)}, bf16[512,512]{1,0:T(8,128)(2,1)S(1)}, u32[]{:S(2)}, u32[]{:S(2)}) collective-permute-start(bf16[512,512]{1,0:T(8,128)(2,1)S(1)} %noise.1), channel_id=1, source_target_pairs={{0,8},{8,0},{1,9},{9,1},{2,10},{10,2},{3,11},{11,3},{4,12},{12,4},... | collective-permute-start | bytes 1572872 | tf_op jit(solution)/shard_map/ppermute | solution.py:278
  143.8 5.2 %collective-permute-start.2 = (bf16[8,72,512]{2,1,0:T(8,128)(2,1)S(1)}, bf16[8,72,512]{2,1,0:T(8,128)(2,1)S(1)}, u32[]{:S(2)}, u32[]{:S(2)}) collective-permute-start(bf16[8,72,512]{2,1,0:T(8,128)(2,1)S(1)} %targets_far.1), channel_id=1, source_target_pairs={{0,8},{8,0},{1,9},{9,1},{2,10},{10,2},{3,11},{11,3},{4,12},{12,4},... | collective-permute-start | bytes 1769480 | tf_op jit(solution)/shard_map/ppermute | solution.py:278

commit v9 on v8

--- a/solution.py
+++ b/solution.py
@@ -132,10 +132,10 @@
     parts, (own, far, expd, tops, lse, part) = refs[:n], refs[n:]
     rows, cols = expd.shape
     half = own.shape[0]
-    pot = jnp.broadcast_to(flat(-log_data - merged(parts)), (8, cols))
+    pot = jnp.broadcast_to(flat(-log_data - merged(parts)), (16, cols))
 
     def rows_at(base, r):
-        return pl.ds(pl.multiple_of(base + r * 8, 8), 8)
+        return pl.ds(pl.multiple_of(base + r * 16, 16), 16)
 
     for flip, score in enumerate((own, far)):
         base = half_at(flip, half)
@@ -148,11 +148,11 @@
             tops[at, :] = top
             low = top - SHIFT
             e = jnp.concatenate([jnp.exp2(tile - low) for tile in tiles], axis=1)
-            expd[at, :] = e
+            expd[at, :] = e.astype(BF16)
             part[at, :] = lane_sum(e)
             return carry
 
-        lax.fori_loop(0, half // 8, body, 0, unroll=8)
+        lax.fori_loop(0, half // 16, body, 0, unroll=4)
     for r in range(rows // 128):
         at = slice(r * 128, (r + 1) * 128)
         turned = tops[at, :].T
@@ -166,11 +166,12 @@
     copies = cols // 128
 
     def body(r, acc):
-        at = pl.ds(pl.multiple_of(r * 8, 8), 8)
+        at = pl.ds(pl.multiple_of(r * 16, 16), 16)
         f = factors[at, :]
-        return acc + expd[at, :] * jnp.concatenate([f] * copies, axis=1)
-
-    acc = lax.fori_loop(0, rows // 8, body, jnp.zeros((8, cols), F32), unroll=8)
+        terms = expd[at, :].astype(F32) * jnp.concatenate([f] * copies, axis=1)
+        return acc + (terms[0:8, :] + terms[8:16, :])
+
+    acc = lax.fori_loop(0, rows // 16, body, jnp.zeros((8, cols), F32), unroll=4)
     sums = jnp.sum(acc, axis=0, keepdims=True)
     count, width = out.shape
     for t in range(count):
@@ -196,15 +197,15 @@
 
 def row_body(count, n, *refs):
     parts, (scale, expd, out, part) = refs[:n], refs[n:]
-    v = jnp.broadcast_to(flat((SCALE / count) / added(parts)), (8, expd.shape[1]))
+    v = jnp.broadcast_to(flat((SCALE / count) / added(parts)), (16, expd.shape[1]))
     rows = expd.shape[0]
 
     def body(r, carry):
-        at = pl.ds(pl.multiple_of(r * 8, 8), 8)
-        part[at, :] = lane_sum(expd[at, :] * v) * scale[at, :]
+        at = pl.ds(pl.multiple_of(r * 16, 16), 16)
+        part[at, :] = lane_sum(expd[at, :].astype(F32) * v) * scale[at, :]
         return carry
 
-    lax.fori_loop(0, rows // 8, body, 0, unroll=8)
+    lax.fori_loop(0, rows // 16, body, 0, unroll=4)
     out[...] = rows_to_lanes(part).astype(out.dtype)
 
 
@@ -231,7 +232,7 @@
         at = slice(r * 128, (r + 1) * 128)
         rows_here = pl.ds(pl.multiple_of(base + r * 128, 128), 128)
         f = jnp.concatenate([factor[rows_here, :]] * (wide // 128), axis=1)
-        w = expd[rows_here, :] * v * f
+        w = expd[rows_here, :].astype(F32) * v * f
         total = jnp.sum(lane_sum(w).T, axis=0, keepdims=True)
         part[r : r + 1, :] = total
         block = jnp.dot(w.astype(BF16), data[...], preferred_element_type=F32).T
@@ -311,7 +312,7 @@
     small = pltpu.VMEM((wide // 128, 128), F32)
     expd, tops, lse = call(
         functools.partial(first_row_body, log_data, 1),
-        (vmem((rows, wide), F32), by_lane, vec_row), 3, [strip], name="first_rows",
+        (vmem((rows, wide), BF16), by_lane, vec_row), 3, [strip], name="first_rows",
     )(parts, score_own, score_far)
     parts = everyone(lse, col_axes)
     sums, scale = call(

time: 172 us -> 173 us (level)
  no operation moved by 1% of the time
where the time goes in v9:
time: 173 us; the launch traced here: 172 us
  blocking collectives  130 us (75%)
  starting transfers between devices  26.6 us (15%)
  Pallas kernels  11.8 us (7%)
  waiting for transfers between devices  3.1 us (2%)
    all_to_all x7, blocking collectives, everyone(): return lax.all_to_all(copies, axes, 0, 0, tiled=True)  91.1 us
    all_to_all x1, blocking collectives, on_device(): got = lax.all_to_all(pieces, COL, 0, 0, tiled=True)  21.8 us
    all_gather x1, blocking collectives, on_device(): lax.all_gather(pair, 'yh', axis=0).reshape(cols_all, slice_width, half)  16.9 us
    all_to_all x1, starting transfers between devices, on_device(): lax.all_to_all(copies, row_axes, 0, 0, tiled=True).reshape(wide, depth)  13.7 us
    ppermute x3, starting transfers between devices, swapped(): return lax.ppermute(val, axis, [(0, 1), (1, 0)])  12.8 us
  transfers between devices with their start and end apart: 4, of which 3 were waited for; matrix products, arithmetic and copies ran while one was open for 0% of the time, Pallas kernels for 2%

profile of v9, /device:TPU:1, one launch (start us, length us, event | category | flops | bytes accessed | tf_op | source)
XLA Modules:
  0.0 172.1 jit_solution(3579884919137941923)
XLA Ops:
  0.0 0.0 copy-start.1
  0.0 0.8 copy-done.1
  0.8 0.0 copy-start
  0.8 1.0 spread.1
  1.8 13.7 %all-to-all-start = ((bf16[32,32,512]{2,1,0:T(8,128)(2,1)}), bf16[32,32,512]{2,1,0:T(8,128)(2,1)S(1)}, u32[]{:S(2)}, u32[]{:S(2)}) async-start(bf16[32,32,512]{2,1,0:T(8,128)(2,1)} %spread.1), calls=%async_computation | async-start | bytes 2097152 | tf_op jit(solution)/shard_map/all_to_all | solution.py:296
  15.5 0.0 copy-done
  15.5 3.2 %collective-permute-start = (bf16[64,512]{1,0:T(8,128)(2,1)S(1)}, bf16[64,512]{1,0:T(8,128)(2,1)S(1)}, u32[]{:S(2)}, u32[]{:S(2)}) collective-permute-start(bf16[64,512]{1,0:T(8,128)(2,1)S(1)} %bitcast.7), channel_id=1, source_target_pairs={{0,1},{1,0},{2,3},{3,2},{4,5},{5,4},{6,7},{7,6},{8,9},{9,8},{10,11... | collective-permute-start | bytes 196616 | tf_op jit(solution)/shard_map/ppermute | solution.py:279
  18.7 2.1 %collective-permute-done.there = bf16[64,512]{1,0:T(8,128)(2,1)S(1)} collective-permute-done((bf16[64,512]{1,0:T(8,128)(2,1)S(1)}, bf16[64,512]{1,0:T(8,128)(2,1)S(1)}, u32[]{:S(2)}, u32[]{:S(2)}) %collective-permute-start) | collective-permute-done | bytes 65568 | tf_op jit(solution)/shard_map/ppermute | solution.py:279
  20.9 16.9 %all-gather.parts = bf16[8,64,512]{2,1,0:T(8,128)(2,1)S(1)} all-gather(bf16[2,64,512]{2,1,0:T(8,128)(2,1)S(1)} %pair.1), channel_id=2, replica_groups=mesh['z'=8,'x'=4,'c'=2,'yh'=4,'yl'=2] {'yh'}, dimensions={0}, use_global_device_ids=true | all-gather | bytes 655360 | tf_op jit(solution)/shard_map/all_gather | solution.py:294
  37.7 0.5 noise.1
  38.2 6.1 %collective-permute-start.1 = (bf16[512,512]{1,0:T(8,128)(2,1)S(1)}, bf16[512,512]{1,0:T(8,128)(2,1)S(1)}, u32[]{:S(2)}, u32[]{:S(2)}) collective-permute-start(bf16[512,512]{1,0:T(8,128)(2,1)S(1)} %noise.1), channel_id=1, source_target_pairs={{0,8},{8,0},{1,9},{9,1},{2,10},{10,2},{3,11},{11,3},{4,12},{12,4},... | collective-permute-start | bytes 1572872 | tf_op jit(solution)/shard_map/ppermute | solution.py:279
  44.3 0.0 all-to-all-done
  44.3 1.1 cost_own.1
  45.4 0.4 collective-permute-done.1.noise
  45.8 1.2 cost_far.1
  47.1 18.7 %all_to_all.45.refs_0_ = f32[32,8,128]{2,1,0:T(8,128)S(1)} all-to-all(f32[32,8,128]{2,1,0:T(8,128)S(1)} %broadcast_in_dim.14), channel_id=1, replica_groups=mesh['z'=8,'x'=4,'c'=2,'yh'=4,'yl'=2] {'z','x'}, dimensions={0} | all-to-all | bytes 262144 | tf_op jit(solution)/shard_map/all_to_all | solution.py:275
  65.8 1.4 first_rows.1
  67.2 13.9 %all_to_all.46.refs_0_ = f32[16,8,128]{2,1,0:T(8,128)S(1)} all-to-all(f32[16,8,128]{2,1,0:T(8,128)S(1)} %broadcast_in_dim.15), channel_id=1, replica_groups=mesh['z'=8,'x'=4,'c'=2,'yh'=4,'yl'=2] {'yh','yl','c'}, dimensions={0} | all-to-all | bytes 131072 | tf_op jit(solution)/shard_map/all_to_all | solution.py:275
  81.1 0.7 first_cols.1
  81.9 11.9 %all_to_all.47.refs_0_ = bf16[32,8,128]{2,1,0:T(8,128)(2,1)S(1)} all-to-all(bf16[32,8,128]{2,1,0:T(8,128)(2,1)S(1)} %broadcast_in_dim.16), channel_id=1, replica_groups=mesh['z'=8,'x'=4,'c'=2,'yh'=4,'yl'=2] {'z','x'}, dimensions={0} | all-to-all | bytes 131072 | tf_op jit(solution)/shard_map/all_to_all | solution.py:275
  93.7 0.8 rows.2
  94.5 11.4 %all_to_all.48.refs_0_ = bf16[16,8,128]{2,1,0:T(8,128)(2,1)S(1)} all-to-all(bf16[16,8,128]{2,1,0:T(8,128)(2,1)S(1)} %broadcast_in_dim.17), channel_id=1, replica_groups=mesh['z'=8,'x'=4,'c'=2,'yh'=4,'yl'=2] {'yh','yl','c'}, dimensions={0} | all-to-all | bytes 65536 | tf_op jit(solution)/shard_map/all_to_all | solution.py:275
  105.9 0.7 cols.2
  106.7 11.8 %all_to_all.49.refs_0_ = bf16[32,8,128]{2,1,0:T(8,128)(2,1)S(1)} all-to-all(bf16[32,8,128]{2,1,0:T(8,128)(2,1)S(1)} %broadcast_in_dim.18), channel_id=1, replica_groups=mesh['z'=8,'x'=4,'c'=2,'yh'=4,'yl'=2] {'z','x'}, dimensions={0} | all-to-all | bytes 131072 | tf_op jit(solution)/shard_map/all_to_all | solution.py:275
  118.5 0.8 rows.3
  119.3 11.5 %all_to_all.50.refs_0_ = bf16[16,8,128]{2,1,0:T(8,128)(2,1)S(1)} all-to-all(bf16[16,8,128]{2,1,0:T(8,128)(2,1)S(1)} %broadcast_in_dim.19), channel_id=1, replica_groups=mesh['z'=8,'x'=4,'c'=2,'yh'=4,'yl'=2] {'yh','yl','c'}, dimensions={0} | all-to-all | bytes 65536 | tf_op jit(solution)/shard_map/all_to_all | solution.py:275
  130.8 0.7 cols.3
  131.5 11.8 %all_to_all.51.refs_0_ = bf16[32,8,128]{2,1,0:T(8,128)(2,1)S(1)} all-to-all(bf16[32,8,128]{2,1,0:T(8,128)(2,1)S(1)} %broadcast_in_dim.20), channel_id=1, replica_groups=mesh['z'=8,'x'=4,'c'=2,'yh'=4,'yl'=2] {'z','x'}, dimensions={0} | all-to-all | bytes 131072 | tf_op jit(solution)/shard_map/all_to_all | solution.py:275
  143.4 1.0 targets_far.1
  144.4 3.5 %collective-permute-start.2 = (bf16[8,72,512]{2,1,0:T(8,128)(2,1)S(1)}, bf16[8,72,512]{2,1,0:T(8,128)(2,1)S(1)}, u32[]{:S(2)}, u32[]{:S(2)}) collective-permute-start(bf16[8,72,512]{2,1,0:T(8,128)(2,1)S(1)} %targets_far.1), channel_id=1, source_target_pairs={{0,8},{8,0},{1,9},{9,1},{2,10},{10,2},{3,11},{11,3},{4,12},{12,4},... | collective-permute-start | bytes 1769480 | tf_op jit(solution)/shard_map/ppermute | solution.py:279
  147.9 1.0 targets_own.1
  148.9 0.6 collective-permute-done.2.far
  149.5 0.1 pack.1
  149.7 21.8 %all_to_all.52.parts = bf16[8,72,512]{2,1,0:T(8,128)(2,1)S(1)} all-to-all(bf16[8,72,512]{2,1,0:T(8,128)(2,1)S(1)} %pack.1), channel_id=1, replica_groups=mesh['z'=8,'x'=4,'c'=2,'yh'=4,'yl'=2] {'yh','yl'}, dimensions={0} | all-to-all | bytes 1179648 | tf_op jit(solution)/shard_map/all_to_all | solution.py:349
  171.4 0.7 finish.1
  (8 shorter events, 0.1 us)
Async XLA Ops:
  0.0 0.8 copy-start.1
  0.8 14.8 %copy-start = (bf16[512,64]{0,1:T(8,128)(2,1)S(1)}, bf16[512,64]{0,1:T(8,128)(2,1)}, u32[]{:S(2)}) copy-start(bf16[512,64]{0,1:T(8,128)(2,1)} %param.2) | copy-start | bytes 196612
  1.8 42.5 %all-to-all-start = ((bf16[32,32,512]{2,1,0:T(8,128)(2,1)}), bf16[32,32,512]{2,1,0:T(8,128)(2,1)S(1)}, u32[]{:S(2)}, u32[]{:S(2)}) async-start(bf16[32,32,512]{2,1,0:T(8,128)(2,1)} %spread.1), calls=%async_computation | async-start | bytes 2097152 | tf_op jit(solution)/shard_map/all_to_all | solution.py:296
  15.5 5.3 %collective-permute-start = (bf16[64,512]{1,0:T(8,128)(2,1)S(1)}, bf16[64,512]{1,0:T(8,128)(2,1)S(1)}, u32[]{:S(2)}, u32[]{:S(2)}) collective-permute-start(bf16[64,512]{1,0:T(8,128)(2,1)S(1)} %bitcast.7), channel_id=1, source_target_pairs={{0,1},{1,0},{2,3},{3,2},{4,5},{5,4},{6,7},{7,6},{8,9},{9,8},{10,11... | collective-permute-start | bytes 196616 | tf_op jit(solution)/shard_map/ppermute | solution.py:279
  38.2 7.6 %collective-permute-start.1 = (bf16[512,512]{1,0:T(8,128)(2,1)S(1)}, bf16[512,512]{1,0:T(8,128)(2,1)S(1)}, u32[]{:S(2)}, u32[]{:S(2)}) collective-permute-start(bf16[512,512]{1,0:T(8,128)(2,1)S(1)} %noise.1), channel_id=1, source_target_pairs={{0,8},{8,0},{1,9},{9,1},{2,10},{10,2},{3,11},{11,3},{4,12},{12,4},... | collective-permute-start | bytes 1572872 | tf_op jit(solution)/shard_map/ppermute | solution.py:279
  144.4 5.2 %collective-permute-start.2 = (bf16[8,72,512]{2,1,0:T(8,128)(2,1)S(1)}, bf16[8,72,512]{2,1,0:T(8,128)(2,1)S(1)}, u32[]{:S(2)}, u32[]{:S(2)}) collective-permute-start(bf16[8,72,512]{2,1,0:T(8,128)(2,1)S(1)} %targets_far.1), channel_id=1, source_target_pairs={{0,8},{8,0},{1,9},{9,1},{2,10},{10,2},{3,11},{11,3},{4,12},{12,4},... | collective-permute-start | bytes 1769480 | tf_op jit(solution)/shard_map/ppermute | solution.py:279
